TPU v7x, 256 devices: a whole 4x4x8 slice. The times are simulated.
256 devices in a mesh: pool: 32 (over y_lo, z, core), tensor: 8 (over x, y_hi).
Axes of the slice: x: 4, y: 4 (y_hi: 2, y_lo: 2; y = y_hi * 2 + y_lo), z: 8, core: 2. Of those that a mesh axis runs over, the one named last changes fastest.
Arguments:
- saved_rows: bfloat16 [65536, 5120], P('pool', 'tensor'), may hold values from -800 to 800
- norm_gain: bfloat16 [5120], replicated, may hold values from 0.099609375 to 1.8984375
- w_key: bfloat16 [5120, 3072], P('pool', 'tensor'), may hold values from -0.078125 to 0.078125
- w_value: bfloat16 [5120, 3072], P('pool', 'tensor'), may hold values from -0.078125 to 0.078125
- req_blocks: int32 [16], replicated, may hold values from 1 to 14, 208 in all
- req_tail: int32 [16], replicated, may hold values from 1 to 128
- group_request: int32 [32], replicated, may hold values from 0 to 31, each once
- owner_table: int32 [16, 14], replicated, may hold values from 0 to 31, as said below
- new_hidden: bfloat16 [128, 2, 5120], P('pool', None, 'tensor'), may hold values from -800 to 800
- queries: bfloat16 [128, 2, 3072], P('pool', None, 'tensor'), may hold values from -200 to 200
- cache_key: bfloat16 [128, 1024, 3072], P('pool', None, 'tensor'), may hold values from -5 to 5
- cache_value: bfloat16 [128, 1024, 3072], P('pool', None, 'tensor'), may hold values from -4 to 4
- cache_len: int32 [128], P('pool'), may hold values from 2 to 1022, as said below
Outputs:
- restored_key: bfloat16 [57344, 3072], P('pool', 'tensor')
- restored_value: bfloat16 [57344, 3072], P('pool', 'tensor')
- decode_out: bfloat16 [128, 2, 3072], P('pool', None, 'tensor')
- new_key: bfloat16 [128, 2, 3072], P('pool', None, 'tensor')
- new_value: bfloat16 [128, 2, 3072], P('pool', None, 'tensor')
Inputs may be any that keep to these rules, and one draw needn't show every extreme that they name: `req_blocks`: they sum to 208; the largest is exactly 14. Each number once; group g restores request group_request[g] when it is below 16, else none. Block i of request r (i < req_blocks[r]) is kept by pool index owner_table[r, i] in its slot r; the numbers of one row differ; entries at i >= req_blocks[r] are unused. `cache_len`: some request has exactly 1022.
All inputs are finite; a program needn't handle non-finite values.
Results may differ from a plain program's by a relative error of at most 0.0056.
Values may be sent and summed in bfloat16 or wider, within the bound.
No kernel may reach another device: no remote copies, remote signals or barrier semaphores. Data moves between devices by JAX's collectives and lax.ppermute only.
A program may use at most 128 MiB of HBM per device.

v0:
```python
import jax
import jax.numpy as jnp
from jax import lax
from jax.sharding import PartitionSpec as P

D = 5120
HEAD_DIM = 128
REQS = 16
BLOCK = 128
GBLK = 14


epsilon = 1e-05


def rotate(values, positions):
    head_count = values.shape[-1] // HEAD_DIM
    half_dim = HEAD_DIM // 2
    shaped = values.reshape(values.shape[:-1] + (head_count, HEAD_DIM))
    frequency = 10000.0 ** (-2.0 * jnp.arange(half_dim, dtype=jnp.float32) / HEAD_DIM)
    angle_rows = positions.astype(jnp.float32)[..., None] * frequency
    cosine = jnp.cos(angle_rows)[..., None, :]
    sine_part = jnp.sin(angle_rows)[..., None, :]
    first_half = shaped[..., :half_dim]
    second = shaped[..., half_dim:]
    turned = jnp.concatenate(
        [first_half * cosine - second * sine_part, second * cosine + first_half * sine_part],
        axis=-1,
    )
    return turned.reshape(values.shape)


def attend(queries, cache_key, cache_value, fresh_key, fresh_value, cache_len):
    local_count, step_count, feature_count = queries.shape
    head_count = feature_count // HEAD_DIM
    context = cache_key.shape[1]
    score_scale = HEAD_DIM ** (-0.5)
    query_heads = queries.reshape(local_count, step_count, head_count, HEAD_DIM)
    cached_heads = cache_key.reshape(local_count, context, head_count, HEAD_DIM)
    cached_scores = (
        jnp.einsum("rshd,rchd->rshc", query_heads, cached_heads, preferred_element_type=jnp.float32)
        * score_scale
    )
    cached_scores = jnp.where(
        jnp.arange(context)[None, None, None, :] < cache_len[:, None, None, None],
        cached_scores,
        -1e30,
    )
    fresh_heads = fresh_key.reshape(local_count, step_count, head_count, HEAD_DIM)
    fresh_scores = (
        jnp.einsum("rshd,rthd->rsht", query_heads, fresh_heads, preferred_element_type=jnp.float32)
        * score_scale
    )
    causal_mask = jnp.arange(step_count)[None, :] <= jnp.arange(step_count)[:, None]
    fresh_scores = jnp.where(causal_mask[None, :, None, :], fresh_scores, -1e30)
    peak_score = jnp.maximum(jnp.max(cached_scores, axis=-1), jnp.max(fresh_scores, axis=-1))
    cached_terms = jnp.exp(cached_scores - peak_score[..., None])
    fresh_terms = jnp.exp(fresh_scores - peak_score[..., None])
    weight_sum = jnp.sum(cached_terms, axis=-1) + jnp.sum(fresh_terms, axis=-1)
    cached_weights = (cached_terms / weight_sum[..., None]).astype(jnp.bfloat16)
    fresh_weights = (fresh_terms / weight_sum[..., None]).astype(jnp.bfloat16)
    cached_values = cache_value.reshape(local_count, context, head_count, HEAD_DIM)
    fresh_values = fresh_value.reshape(local_count, step_count, head_count, HEAD_DIM)
    output = jnp.einsum(
        "rshc,rchd->rshd", cached_weights, cached_values, preferred_element_type=jnp.float32
    )
    output = output + jnp.einsum(
        "rsht,rthd->rshd", fresh_weights, fresh_values, preferred_element_type=jnp.float32
    )
    return output.reshape(local_count, step_count, feature_count).astype(jnp.bfloat16)


def shards(
    saved_rows,
    norm_gain,
    w_key,
    w_value,
    req_blocks,
    req_tail,
    group_request,
    owner_table,
    new_hidden,
    queries,
    cache_key,
    cache_value,
    cache_len,
):
    slice_width = saved_rows.shape[1]
    owner_index = lax.axis_index("pool")
    storage = saved_rows.reshape(REQS, BLOCK, slice_width)
    block_rank = jnp.arange(GBLK, dtype=jnp.int32)
    present = group_request < REQS
    chosen = jnp.minimum(group_request, REQS - 1)
    counted = block_rank[None, :] < jnp.take(req_blocks, chosen)[:, None]
    holding = (
        jnp.any((jnp.take(owner_table, chosen, axis=0) == owner_index) & counted, axis=1) & present
    )
    outgoing = jnp.where(
        holding[:, None, None], jnp.take(storage, chosen, axis=0), jnp.zeros((), jnp.bfloat16)
    )
    wanted = group_request[owner_index]
    target = jnp.minimum(wanted, REQS - 1)
    senders = owner_table[target]
    token_count = jnp.where(wanted < REQS, (req_blocks[target] - 1) * BLOCK + req_tail[target], 0)
    position = jnp.arange(GBLK * BLOCK, dtype=jnp.int32)
    live_rows = position < token_count
    incoming = lax.all_to_all(outgoing, "pool", split_axis=0, concat_axis=0, tiled=True)
    compact = jnp.take(incoming, senders, axis=0).reshape(GBLK * BLOCK, slice_width)
    compact = jnp.where(live_rows[:, None], compact, jnp.zeros((), jnp.bfloat16))
    gain_wide = norm_gain.astype(jnp.float32)
    full_rows = lax.all_gather(compact, "tensor", axis=1, tiled=True)
    wide_rows = full_rows.astype(jnp.float32)
    squares = jnp.sum(wide_rows * wide_rows, axis=1)
    scaled = (wide_rows * gain_wide).astype(jnp.bfloat16)
    key_sum = jnp.dot(
        scaled,
        lax.all_gather(w_key, "pool", axis=0, tiled=True),
        preferred_element_type=jnp.float32,
    )
    value_sum = jnp.dot(
        scaled,
        lax.all_gather(w_value, "pool", axis=0, tiled=True),
        preferred_element_type=jnp.float32,
    )
    inverse = lax.rsqrt(squares / D + epsilon)
    restored_key = rotate(key_sum * inverse[:, None], position).astype(jnp.bfloat16)
    restored_value = (value_sum * inverse[:, None]).astype(jnp.bfloat16)
    local_count, step_count = (new_hidden.shape[0], new_hidden.shape[1])
    tokens = lax.all_gather(new_hidden, "tensor", axis=2, tiled=True).reshape(
        local_count * step_count, D
    )
    token_wide = tokens.astype(jnp.float32)
    token_inverse = lax.rsqrt(jnp.sum(token_wide * token_wide, axis=1) / D + epsilon)
    token_scaled = (token_wide * gain_wide).astype(jnp.bfloat16)
    head_width = w_key.shape[1]
    columns = lax.all_to_all(token_scaled, "pool", split_axis=1, concat_axis=0, tiled=True)
    paired = jnp.concatenate([w_key, w_value], axis=1)
    projected = lax.psum_scatter(
        jnp.dot(columns, paired, preferred_element_type=jnp.float32),
        "pool",
        scatter_dimension=0,
        tiled=True,
    )
    token_key = projected[:, :head_width]
    token_value = projected[:, head_width:]
    positions = cache_len[:, None] + jnp.arange(step_count, dtype=jnp.int32)[None, :]
    new_key = rotate(
        (token_key * token_inverse[:, None]).reshape(local_count, step_count, head_width), positions
    ).astype(jnp.bfloat16)
    new_value = (
        (token_value * token_inverse[:, None])
        .reshape(local_count, step_count, head_width)
        .astype(jnp.bfloat16)
    )
    decode_out = attend(queries, cache_key, cache_value, new_key, new_value, cache_len)
    return (restored_key, restored_value, decode_out, new_key, new_value)


def solution(mesh):
    return jax.shard_map(
        shards,
        mesh=mesh,
        in_specs=(
            P("pool", "tensor"),
            P(),
            P("pool", "tensor"),
            P("pool", "tensor"),
            P(),
            P(),
            P(),
            P(),
            P("pool", None, "tensor"),
            P("pool", None, "tensor"),
            P("pool", None, "tensor"),
            P("pool", None, "tensor"),
            P("pool"),
        ),
        out_specs=(
            P("pool", "tensor"),
            P("pool", "tensor"),
            P("pool", None, "tensor"),
            P("pool", None, "tensor"),
            P("pool", None, "tensor"),
        ),
        check_vma=False,
    )
```

profile of v0, /device:TPU:1, one launch (start us, length us, event | category | flops | bytes accessed | tf_op | source)
XLA Modules:
  0.0 565.4 jit_solution(15046189075297222952)
XLA Ops:
  8.0 0.0 copy-start
  8.0 29.1 %all_gather.15 = bf16[4,2,5120]{2,1,0:T(2,128)(2,1)S(1)} all-gather(bf16[4,2,640]{2,1,0:T(2,128)(2,1)} %param.21), channel_id=1, replica_groups=mesh['pool'=32,'tensor'=8] {'tensor'}, dimensions={2}, use_global_device_ids=true | all-gather | bytes 92160 | tf_op jit(solution)/shard_map/all_gather | solution.py:129
  37.1 0.2 reshape.263
  37.3 0.8 mul.214
  38.1 0.8 fusion.23
  38.9 16.7 %all-to-all-start.1 = ((bf16[8,32,160]{2,0,1:T(8,128)(2,1)}), bf16[8,32,160]{2,0,1:T(8,128)(2,1)S(1)}, u32[]{:S(2)}, u32[]{:S(2)}) async-start(bf16[8,32,160]{2,0,1:T(8,128)(2,1)} %fusion.23), calls=%async_computation.1 | async-start | bytes 262144 | tf_op jit(solution)/shard_map/all_to_all | solution.py:136
  55.5 0.7 compare_and_fusion.1
  56.2 0.0 copy-start.3
  56.2 0.0 copy-start.2
  56.2 0.0 copy-start.9
  56.3 3.5 gather_fusion.2
  59.8 0.0 copy-done.3
  59.8 0.6 gather_fusion
  60.4 0.7 gather_fusion.1
  61.1 0.2 fusion.33
  61.3 5.6 select_select_fusion
  66.9 0.0 all-to-all-done.1
  66.9 8.5 %all-to-all-start = ((bf16[32,128,640]{2,1,0:T(8,128)(2,1)}), bf16[32,128,640]{2,1,0:T(8,128)(2,1)}, u32[]{:S(2)}, u32[]{:S(2)}) async-start(bf16[32,128,640]{2,1,0:T(8,128)(2,1)} %select_select_fusion), calls=%async_computation | async-start | bytes 10485760 | tf_op jit(solution)/shard_map/all_to_all | solution.py:107
  75.4 0.0 reduce-scatter.2.cloned.1.call-start
  75.5 0.0 copy-done.4
  75.5 1.1 fusion.24
  76.6 0.0 reduce-scatter.2.cloned.1.call-update
  76.7 0.0 all-gather.4.cloned.1.call-start
  76.7 0.6 dynamic_slice.12
  78.6 0.6 dynamic_slice.13
  79.2 0.6 dynamic_slice.14
  81.2 0.1 broadcast_bitcast_fusion
  81.2 114.3 %all-to-all-done = bf16[32,128,640]{2,1,0:T(8,128)(2,1)} async-done(((bf16[32,128,640]{2,1,0:T(8,128)(2,1)}), bf16[32,128,640]{2,1,0:T(8,128)(2,1)}, u32[]{:S(2)}, u32[]{:S(2)}) %all-to-all-start) | async-done | bytes 5242912 | tf_op jit(solution)/shard_map/all_to_all | solution.py:107
  195.5 3.5 gather_fusion.3
  199.0 0.0 copy-start.6
  199.1 2.4 fusion.15
  201.4 0.0 all-gather.4.cloned.1.call-update
  201.4 0.0 all-gather.6.cloned.1.call-start
  201.5 0.5 all-gather.6.cloned.1.call-update
  202.0 0.2 all-gather.8.cloned.1.call-start
  202.3 0.3 all-gather.8.cloned.1.call-update
  202.6 0.2 multiply_reduce_fusion
  202.8 4.7 copy.37
  207.5 4.8 copy.30
  212.2 0.1 rsqrt.19
  212.3 0.1 add_convert_fusion.1
  212.4 0.1 iota_compare_fusion
  212.5 0.1 multiply_cosine_fusion.1
  212.6 3.0 fusion.44
  215.6 1.7 multiply_cosine_fusion
  217.3 4.4 reduce-scatter.2.cloned.1.call-done
  221.7 0.8 fusion.34
  222.5 0.6 convert_element_type.98
  223.1 0.1 fusion.43
  223.2 0.2 fusion.45
  223.5 0.2 fusion.29
  223.7 0.7 fusion.51
  224.4 2.9 convolution_bitcast_fusion.1
  227.3 0.8 fusion.22
  228.1 177.0 %all-gather.4.cloned.1.call-done = bf16[1792,5120]{1,0:T(8,128)(2,1)} async-done(((bf16[1792,640]{1,0:T(8,128)(2,1)}), bf16[1792,5120]{1,0:T(8,128)(2,1)}) %all-gather.4.cloned.1.call-update) | async-done | bytes 18350096 | tf_op jit(solution)/shard_map/all_gather | solution.py:111
  405.1 7.5 %fusion.1 = f32[1792]{0:T(1024)S(1)} fusion(bf16[1792,5120]{1,0:T(8,128)(2,1)} %all-gather.4.cloned.1.call-done), kind=kLoop, calls=%fused_computation.7 | loop fusion | flops 27523328 | bytes 18357248 | tf_op jit(solution)/shard_map/reduce_sum | solution.py:113
  412.6 60.0 %all-gather.6.cloned.1.call-done = bf16[5120,384]{1,0:T(8,128)(2,1)} async-done(((bf16[160,384]{1,0:T(8,128)(2,1)}), bf16[5120,384]{1,0:T(8,128)(2,1)}) %all-gather.6.cloned.1.call-update) | async-done | bytes 3932176 | tf_op jit(solution)/shard_map/all_gather | solution.py:117
  472.6 14.4 %fusion.6 = f32[1792,384]{0,1:T(8,128)} fusion(bf16[5120,384]{1,0:T(8,128)(2,1)} %all-gather.6.cloned.1.call-done, bf16[1792,5120]{1,0:T(8,128)(2,1)} %all-gather.4.cloned.1.call-done, f32[5120]{0:T(1024)S(1)} %convert_element_type.80, f32[1792]{0:T(1024)S(1)} %add_rsqrt_fusion), kind=kOutput, calls=%fused_computation.11 | convolution fusion | flops 7074643968 | bytes 25062400 | tf_op jit(solution)/shard_map/dot_general | solution.py:115
  487.0 2.1 subtract_convert_fusion
  489.0 0.1 pad_maximum_fusion
  489.1 1.5 copy.41
  490.7 50.2 %all-gather.8.cloned.1.call-done = bf16[5120,384]{1,0:T(8,128)(2,1)} async-done(((bf16[160,384]{1,0:T(8,128)(2,1)}), bf16[5120,384]{1,0:T(8,128)(2,1)}) %all-gather.8.cloned.1.call-update) | async-done | bytes 3932176 | tf_op jit(solution)/shard_map/all_gather | solution.py:122
  540.9 14.4 %fusion.12 = bf16[1792,384]{0,1:T(8,128)(2,1)} fusion(bf16[5120,384]{1,0:T(8,128)(2,1)} %all-gather.8.cloned.1.call-done, bf16[1792,5120]{1,0:T(8,128)(2,1)} %all-gather.4.cloned.1.call-done, f32[5120]{0:T(1024)S(1)} %convert_element_type.80, f32[1792]{0:T(1024)S(1)} %add_rsqrt_fusion), kind=kOutput, calls=%fused_computation.13 | convolution fusion | flops 7075332096 | bytes 23686144 | tf_op jit(solution)/shard_map/dot_general | solution.py:120
  555.3 2.5 copy.42
  (34 shorter events, 0.2 us)
Async XLA Ops:
  8.0 48.2 %copy-start = (bf16[2048,640]{1,0:T(8,128)(2,1)S(1)}, bf16[2048,640]{1,0:T(8,128)(2,1)}, u32[]{:S(2)}) copy-start(bf16[2048,640]{1,0:T(8,128)(2,1)} %param.13) | copy-start | bytes 7864324
  38.9 28.0 %all-to-all-start.1 = ((bf16[8,32,160]{2,0,1:T(8,128)(2,1)}), bf16[8,32,160]{2,0,1:T(8,128)(2,1)S(1)}, u32[]{:S(2)}, u32[]{:S(2)}) async-start(bf16[8,32,160]{2,0,1:T(8,128)(2,1)} %fusion.23), calls=%async_computation.1 | async-start | bytes 262144 | tf_op jit(solution)/shard_map/all_to_all | solution.py:136
  56.2 3.6 copy-start.3
  56.2 4.1 copy-start.2
  56.2 5.0 copy-start.9
  66.9 8.6 %copy-start.4 = (bf16[160,384]{1,0:T(8,128)(2,1)S(1)}, bf16[160,384]{1,0:T(8,128)(2,1)}, u32[]{:S(2)}) copy-start(bf16[160,384]{1,0:T(8,128)(2,1)} %param.15) | copy-start | bytes 368644
  66.9 8.6 %copy-start.5 = (bf16[160,384]{1,0:T(8,128)(2,1)S(1)}, bf16[160,384]{1,0:T(8,128)(2,1)}, u32[]{:S(2)}) copy-start(bf16[160,384]{1,0:T(8,128)(2,1)} %param.16) | copy-start | bytes 368644
  66.9 12.3 %copy-start.10 = (s32[16]{0:T(128)S(1)}, s32[16]{0:T(128)}, u32[]{:S(2)}) copy-start(s32[16]{0:T(128)} %param.18) | copy-start | bytes 196
  66.9 128.6 %all-to-all-start = ((bf16[32,128,640]{2,1,0:T(8,128)(2,1)}), bf16[32,128,640]{2,1,0:T(8,128)(2,1)}, u32[]{:S(2)}, u32[]{:S(2)}) async-start(bf16[32,128,640]{2,1,0:T(8,128)(2,1)} %select_select_fusion), calls=%async_computation | async-start | bytes 10485760 | tf_op jit(solution)/shard_map/all_to_all | solution.py:107
  75.4 146.3 %reduce-scatter.2.cloned.1.call-start = ((), (), s32[]{:S(2)}) async-start(), calls=%async_computation.6 | async-start | bytes 811008 | tf_op jit(solution)/shard_map/reduce_scatter | solution.py:138
  76.7 328.4 %all-gather.4.cloned.1.call-start = ((), (), s32[]{:S(2)}) async-start(), calls=%async_computation.3 | async-start | bytes 20643840 | tf_op jit(solution)/shard_map/all_gather | solution.py:111
  199.0 3.8 copy-start.6
  201.4 271.1 %all-gather.6.cloned.1.call-start = ((), (), s32[]{:S(2)}) async-start(), calls=%async_computation.4 | async-start | bytes 4055040 | tf_op jit(solution)/shard_map/all_gather | solution.py:117
  202.0 338.9 %all-gather.8.cloned.1.call-start = ((), (), s32[]{:S(2)}) async-start(), calls=%async_computation.5 | async-start | bytes 4055040 | tf_op jit(solution)/shard_map/all_gather | solution.py:122
  207.5 4.8 copy-start.8
  207.5 5.1 copy-start.7
  540.9 16.9 %copy-start.1 = (bf16[2048,640]{1,0:T(8,128)(2,1)S(1)}, bf16[2048,640]{1,0:T(8,128)(2,1)}, u32[]{:S(2)}) copy-start(bf16[2048,640]{1,0:T(8,128)(2,1)} %param.13) | copy-start | bytes 7864324
Sparse Core Ops, SparseCore 0:
  79.3 142.3 reduce-scatter.1
Sparse Core Ops, SparseCore 1:
  201.5 203.5 all-gather.3
  406.8 65.7 all-gather.5
  474.3 66.5 all-gather.7
where the time goes:
time: 566 us; the launch traced here: 565 us
  waiting for transfers between devices  407 us (72%)
  matrix products  36.7 us (6%)
  blocking collectives  29.1 us (5%)
  starting transfers between devices  25.5 us (5%)
  local copies, waits for them, and re-layouts  25.4 us (4%)
  other arithmetic  23.4 us (4%)
  between operations  18.5 us (3%)
    all_gather x1, waiting for transfers between devices, shards(): full_rows = lax.all_gather(compact, 'tensor', axis=1, tiled=True)  177 us
    all_to_all x1, waiting for transfers between devices, shards(): lax.all_to_all(outgoing, 'pool', split_axis=0, concat_axis=0, tiled=True)  114 us
    all_gather x1, waiting for transfers between devices, shards(): lax.all_gather(w_key, 'pool', axis=0, tiled=True)  60 us
    all_gather x1, waiting for transfers between devices, shards(): lax.all_gather(w_value, 'pool', axis=0, tiled=True)  50.2 us
    all_gather x1, blocking collectives, shards(): lax.all_gather(new_hidden, 'tensor', axis=2, tiled=True)  29.1 us
    all_to_all x1, starting transfers between devices, shards(): lax.all_to_all(token_scaled, 'pool', split_axis=1, concat_axis=0, tiled=T...  16.7 us
    dot_general x1, matrix products, shards(): jnp.dot(scaled, lax.all_gather(w_key, 'pool', axis=0, tiled=True), prefer...  14.4 us
    dot_general x1, matrix products, shards(): jnp.dot(scaled, lax.all_gather(w_value, 'pool', axis=0, tiled=True), pref...  14.4 us
  transfers between devices with their start and end apart: 6, of which 5 were waited for; matrix products, arithmetic and copies ran while one was open for 12% of the time, Pallas kernels for 0%

commit v1 on v0

v1 whole, which is shorter than its diff:
```python
import jax
import jax.numpy as jnp
from jax import lax
from jax.experimental import pallas as pl
from jax.experimental.pallas import tpu as pltpu
from jax.sharding import PartitionSpec as P

D = 5120
HEAD_DIM = 128
REQS = 16
BLOCK = 128
BLOCKS = 208
GBLK = 14
N_POOL = 32
N_TENSOR = 8
SLICE = D // N_TENSOR
SHARE = BLOCK // N_POOL
ROWS = BLOCKS * SHARE
SLOT = GBLK * SHARE
TOKENS = 16
X_FIRST = 208
KEPT = REQS * SLOT


epsilon = 1e-05


def turn_table(positions):
    half_dim = HEAD_DIM // 2
    frequency = 10000.0 ** (-2.0 * jnp.arange(half_dim, dtype=jnp.float32) / HEAD_DIM)
    angle_rows = positions.astype(jnp.float32)[..., None] * frequency
    cosine, sine_part = jnp.cos(angle_rows), jnp.sin(angle_rows)
    return jnp.concatenate([cosine, cosine], axis=-1), jnp.concatenate([-sine_part, sine_part], axis=-1)


def add_slices(steps, source_ref, gain_ref, weight_ref, pieces_of, scaled_ref, total_ref, squares_ref, begun):
    for step in steps:
        source = source_ref[step]
        gain = gain_ref[source]
        begin = 0
        for piece in pieces_of(step):
            end = begin + piece.shape[0]
            wide = piece.astype(jnp.float32)
            square = wide * wide
            lanes = square[:, :128]
            for low in range(128, SLICE, 128):
                lanes = lanes + square[:, low : low + 128]
            squares_ref[begin:end, :] = squares_ref[begin:end, :] + lanes if begun else lanes
            scaled_ref[begin:end, :] = (wide * gain).astype(jnp.bfloat16)
            begin = end
        part = jnp.dot(scaled_ref[...], weight_ref[source], preferred_element_type=jnp.float32)
        total_ref[:begin, :] = total_ref[:begin, :] + part if begun else part
        begun = True


def near_kernel(
    source_ref,
    near_ref,
    near_across_ref,
    two_ref,
    before_ref,
    after_ref,
    gain_ref,
    weight_ref,
    total_ref,
    squares_ref,
    scaled_ref,
):
    low_rows = two_ref.shape[0] // 2
    top = total_ref.shape[0] - low_rows

    def pieces_of(step):
        offset, across = step // 2, step % 2
        upper = (near_across_ref if across else near_ref)[offset * top : (offset + 1) * top, :]
        lower = (two_ref, before_ref, after_ref)[offset][across * low_rows : (across + 1) * low_rows, :]
        return upper, lower

    add_slices(range(6), source_ref, gain_ref, weight_ref, pieces_of, scaled_ref, total_ref, squares_ref, False)


def far_kernel(
    source_ref,
    start_ref,
    count_ref,
    far_ref,
    far_across_ref,
    two_far_ref,
    gain_ref,
    weight_ref,
    begun_ref,
    begun_squares_ref,
    live_ref,
    cosine_ref,
    sine_ref,
    out_ref,
    fresh_ref,
    scaled_ref,
    total_ref,
    squares_ref,
):
    rows, columns = begun_ref.shape
    low_rows = two_far_ref.shape[0] // 2
    total_ref[:rows, :] = begun_ref[...]
    total_ref[rows:, :] = jnp.zeros((KEPT - rows, columns), jnp.float32)
    squares_ref[...] = begun_squares_ref[...]

    def pieces_of(step):
        across = step % 2
        upper = (far_across_ref if across else far_ref)[...]
        return upper, two_far_ref[across * low_rows : (across + 1) * low_rows, :]

    add_slices(range(6, 8), source_ref, gain_ref, weight_ref, pieces_of, scaled_ref, total_ref, squares_ref, True)
    inverse = lax.rsqrt(jnp.sum(squares_ref[...], axis=1, keepdims=True) / D + epsilon) * live_ref[...]
    cosine, sine_part = cosine_ref[...], sine_ref[...]
    for low in range(0, columns, HEAD_DIM):
        one = total_ref[:rows, low : low + HEAD_DIM] * inverse
        if low < columns // 2:
            one = one * cosine + pltpu.roll(one, HEAD_DIM // 2, 1) * sine_part
        total_ref[:rows, low : low + HEAD_DIM] = one
    fresh_ref[...] = total_ref[ROWS : ROWS + TOKENS, :].astype(jnp.bfloat16)

    def send(group, carry):
        start = start_ref[group]
        tile = start // 8
        window = total_ref[pl.ds(pl.multiple_of(tile * 8, 8), SLOT + 8), :]
        mine = jnp.where(start == tile * 8, window[:SLOT], window[SHARE : SHARE + SLOT])
        line = lax.broadcasted_iota(jnp.int32, (SLOT, columns), 0)
        out_ref[group] = jnp.where(line < count_ref[group], mine, 0.0).astype(jnp.bfloat16)
        return carry

    lax.fori_loop(0, N_POOL, send, 0)


def project(sources, starts, counts, pieces, weights, gain_wide, live, cosine, sine_part):
    near, far, near_across, far_across, two, two_before, two_after, two_far = pieces
    rows = live.shape[0]
    columns = weights.shape[2]
    whole = pl.BlockSpec(memory_space=pltpu.VMEM)
    numbers = pl.BlockSpec(memory_space=pltpu.SMEM)
    total, squares = pl.pallas_call(
        near_kernel,
        out_shape=(
            jax.ShapeDtypeStruct((rows, columns), jnp.float32),
            jax.ShapeDtypeStruct((rows, 128), jnp.float32),
        ),
        in_specs=[numbers] + [whole] * 7,
        out_specs=(whole, whole),
        scratch_shapes=[pltpu.VMEM((rows, SLICE), jnp.bfloat16)],
        compiler_params=pltpu.CompilerParams(vmem_limit_bytes=40 * 1024 * 1024),
        cost_estimate=pl.CostEstimate(
            flops=3 * rows * D * columns // 2, bytes_accessed=2 * D * (rows + columns), transcendentals=0
        ),
    )(sources, near, near_across, two, two_before, two_after, gain_wide, weights)
    return pl.pallas_call(
        far_kernel,
        out_shape=(
            jax.ShapeDtypeStruct((N_POOL, SLOT, columns), jnp.bfloat16),
            jax.ShapeDtypeStruct((TOKENS, columns), jnp.bfloat16),
        ),
        in_specs=[numbers] * 3 + [whole] * 10,
        out_specs=(whole, whole),
        scratch_shapes=[
            pltpu.VMEM((rows, SLICE), jnp.bfloat16),
            pltpu.VMEM((KEPT, columns), jnp.float32),
            pltpu.VMEM((rows, 128), jnp.float32),
        ],
        compiler_params=pltpu.CompilerParams(vmem_limit_bytes=40 * 1024 * 1024),
        cost_estimate=pl.CostEstimate(
            flops=rows * D * columns // 2, bytes_accessed=D * (rows + columns), transcendentals=0
        ),
    )(
        sources, starts, counts, far, far_across, two_far, gain_wide, weights, total, squares, live, cosine, sine_part
    )


def pick_rows(index, table):
    chosen = (index[:, None] == jnp.arange(table.shape[0], dtype=jnp.int32)[None, :]).astype(jnp.bfloat16)
    return jnp.dot(chosen, table, preferred_element_type=jnp.float32).astype(jnp.bfloat16)


def along_x(values, step):
    pairs = [(s, ((s // 2 + step) % 4) * 2 + s % 2) for s in range(N_TENSOR)]
    return lax.ppermute(values, "tensor", pairs)


def across_y(values):
    return lax.ppermute(values, "tensor", [(s, s ^ 1) for s in range(N_TENSOR)])


def far_x(before, after, rows):
    return jnp.concatenate([along_x(before[:rows], 1), along_x(after[rows:], -1)], axis=0)


def gather_rows(own):
    upper, lower = own[:X_FIRST], own[X_FIRST:]
    other = across_y(lower)
    before, after = along_x(upper, 1), along_x(upper, -1)
    other, before, after = lax.optimization_barrier((other, before, after))
    near = jnp.concatenate([upper, before, after], axis=0)
    two = jnp.concatenate([lower, other], axis=0)
    far = far_x(before, after, X_FIRST // 2)
    two_before, two_after = along_x(two, 1), along_x(two, -1)
    near_across = across_y(near)
    far, two_before, two_after, near_across = lax.optimization_barrier((far, two_before, two_after, near_across))
    far_across = across_y(far)
    two_far = far_x(two_before, two_after, lower.shape[0])
    return near, far, near_across, far_across, two, two_before, two_after, two_far


def shards(
    saved_rows,
    norm_gain,
    w_key,
    w_value,
    req_blocks,
    req_tail,
    group_request,
    owner_table,
    new_hidden,
    queries,
    cache_key,
    cache_value,
    cache_len,
):
    slice_width = saved_rows.shape[1]
    head_width = w_key.shape[1]
    pool_index = lax.axis_index("pool")
    tensor_index = lax.axis_index("tensor")
    x_index, y_index = tensor_index // 2, tensor_index % 2
    gain_wide = norm_gain.astype(jnp.float32).reshape(N_TENSOR, 1, SLICE)
    order = jnp.stack([x_index, (x_index + 3) % 4, (x_index + 1) % 4, (x_index + 2) % 4]).astype(jnp.int32)
    sources = jnp.stack([order * 2 + y_index, order * 2 + 1 - y_index], axis=1).reshape(-1)

    slot = jnp.arange(REQS, dtype=jnp.int32)
    inside = jnp.arange(SHARE, dtype=jnp.int32)
    tiles = saved_rows.reshape(REQS, N_POOL // 2, 2 * SHARE, slice_width).transpose(1, 0, 2, 3)
    tiles = tiles.reshape(N_POOL // 2, REQS * 2 * SHARE, slice_width)
    line = jnp.arange(REQS * 2 * SHARE, dtype=jnp.int32)
    half = REQS * SHARE
    away = (line % half) // SHARE * (2 * SHARE) + line // half * SHARE + line % SHARE
    away = (away[:, None] == line[None, :]).astype(jnp.bfloat16)
    spread = jnp.einsum("ab,qbc->qac", away, tiles, preferred_element_type=jnp.float32).astype(jnp.bfloat16)
    spread = spread.reshape(N_POOL, REQS * SHARE, slice_width)
    incoming = lax.all_to_all(spread, "pool", split_axis=0, concat_axis=0, tiled=True)

    local_count, step_count = (new_hidden.shape[0], new_hidden.shape[1])
    tokens = local_count * step_count
    ends = jnp.cumsum(req_blocks)
    starts = ends - req_blocks
    count = jnp.arange(BLOCKS, dtype=jnp.int32)
    member = (count[:, None] >= starts[None, :]) & (count[:, None] < ends[None, :])
    request = jnp.sum(jnp.where(member, slot[None, :], 0), axis=1)
    inner = count - jnp.sum(jnp.where(member, starts[None, :], 0), axis=1)
    length = jnp.sum(jnp.where(member, ((req_blocks - 1) * BLOCK + req_tail)[None, :], 0), axis=1)
    at = (request * GBLK + inner)[:, None] == jnp.arange(REQS * GBLK, dtype=jnp.int32)[None, :]
    owner = jnp.sum(jnp.where(at, owner_table.reshape(1, -1), 0), axis=1)
    my_rows = ((owner * REQS + request)[:, None] * SHARE + inside).reshape(-1)
    position = ((inner * BLOCK + pool_index * SHARE)[:, None] + inside).reshape(-1)
    live = (position < jnp.repeat(length, SHARE)).astype(jnp.float32)
    token_position = (cache_len[:, None] + jnp.arange(step_count, dtype=jnp.int32)[None, :]).reshape(-1)
    position = jnp.concatenate([position, token_position, token_position])
    live = jnp.concatenate([live, jnp.ones((TOKENS,), jnp.float32)])[:, None]
    cosine, sine_part = turn_table(position)

    holder = (group_request[:, None] == slot[None, :]).astype(jnp.int32)
    group_start = jnp.sum(holder * starts[None, :], axis=1) * SHARE
    group_rows = jnp.sum(holder * req_blocks[None, :], axis=1) * SHARE
    incoming, my_rows, live, cosine, sine_part, group_start, group_rows = lax.optimization_barrier(
        (incoming, my_rows, live, cosine, sine_part, group_start, group_rows)
    )

    paired = jnp.concatenate([w_key, w_value], axis=1)
    paired, incoming = lax.optimization_barrier((paired, incoming))
    weights = lax.all_gather(paired, "pool", axis=0, tiled=True).reshape(N_TENSOR, SLICE, 2 * head_width)
    token_rows = jnp.concatenate(
        [new_hidden.reshape(tokens, slice_width), jnp.zeros((TOKENS - tokens, slice_width), jnp.bfloat16)], axis=0
    )
    own = pick_rows(my_rows, incoming.reshape(N_POOL * REQS * SHARE, slice_width))
    own = jnp.concatenate([own, token_rows], axis=0)
    outgoing, fresh = project(
        sources, group_start, group_rows, gather_rows(own), weights, gain_wide, live, cosine, sine_part
    )
    arrived = lax.all_to_all(outgoing, "pool", split_axis=0, concat_axis=0, tiled=True)
    pairs = arrived.reshape(N_POOL, GBLK // 2, 2 * SHARE, 2 * head_width).transpose(1, 0, 2, 3)
    pairs = pairs.reshape(GBLK // 2, 2 * BLOCK, 2 * head_width)
    line = jnp.arange(2 * BLOCK, dtype=jnp.int32)
    home = (line % BLOCK) // SHARE * (2 * SHARE) + line // BLOCK * SHARE + line % SHARE
    home = (home[:, None] == line[None, :]).astype(jnp.bfloat16)

    def in_order(part):
        ordered = jnp.einsum("ab,ibc->iac", home, part, preferred_element_type=jnp.float32)
        return ordered.astype(jnp.bfloat16).reshape(GBLK * BLOCK, head_width)

    restored_key = in_order(pairs[..., :head_width])
    restored_value = in_order(pairs[..., head_width:])
    fresh = fresh[:tokens].reshape(local_count, step_count, 2 * head_width)
    new_key, new_value = fresh[..., :head_width], fresh[..., head_width:]
    decode_out = attend(queries, cache_key, cache_value, new_key, new_value, cache_len)
    return (restored_key, restored_value, decode_out, new_key, new_value)


def attend(queries, cache_key, cache_value, fresh_key, fresh_value, cache_len):
    local_count, step_count, feature_count = queries.shape
    head_count = feature_count // HEAD_DIM
    context = cache_key.shape[1]
    score_scale = HEAD_DIM ** (-0.5)
    query_heads = queries.reshape(local_count, step_count, head_count, HEAD_DIM)
    cached_heads = cache_key.reshape(local_count, context, head_count, HEAD_DIM)
    cached_scores = (
        jnp.einsum("rshd,rchd->rshc", query_heads, cached_heads, preferred_element_type=jnp.float32)
        * score_scale
    )
    cached_scores = jnp.where(
        jnp.arange(context)[None, None, None, :] < cache_len[:, None, None, None],
        cached_scores,
        -1e30,
    )
    fresh_heads = fresh_key.reshape(local_count, step_count, head_count, HEAD_DIM)
    fresh_scores = (
        jnp.einsum("rshd,rthd->rsht", query_heads, fresh_heads, preferred_element_type=jnp.float32)
        * score_scale
    )
    causal_mask = jnp.arange(step_count)[None, :] <= jnp.arange(step_count)[:, None]
    fresh_scores = jnp.where(causal_mask[None, :, None, :], fresh_scores, -1e30)
    peak_score = jnp.maximum(jnp.max(cached_scores, axis=-1), jnp.max(fresh_scores, axis=-1))
    cached_terms = jnp.exp(cached_scores - peak_score[..., None])
    fresh_terms = jnp.exp(fresh_scores - peak_score[..., None])
    weight_sum = jnp.sum(cached_terms, axis=-1) + jnp.sum(fresh_terms, axis=-1)
    cached_weights = (cached_terms / weight_sum[..., None]).astype(jnp.bfloat16)
    fresh_weights = (fresh_terms / weight_sum[..., None]).astype(jnp.bfloat16)
    cached_values = cache_value.reshape(local_count, context, head_count, HEAD_DIM)
    fresh_values = fresh_value.reshape(local_count, step_count, head_count, HEAD_DIM)
    output = jnp.einsum(
        "rshc,rchd->rshd", cached_weights, cached_values, preferred_element_type=jnp.float32
    )
    output = output + jnp.einsum(
        "rsht,rthd->rshd", fresh_weights, fresh_values, preferred_element_type=jnp.float32
    )
    return output.reshape(local_count, step_count, feature_count).astype(jnp.bfloat16)


def solution(mesh):
    return jax.shard_map(
        shards,
        mesh=mesh,
        in_specs=(
            P("pool", "tensor"),
            P(),
            P("pool", "tensor"),
            P("pool", "tensor"),
            P(),
            P(),
            P(),
            P(),
            P("pool", None, "tensor"),
            P("pool", None, "tensor"),
            P("pool", None, "tensor"),
            P("pool", None, "tensor"),
            P("pool"),
        ),
        out_specs=(
            P("pool", "tensor"),
            P("pool", "tensor"),
            P("pool", None, "tensor"),
            P("pool", None, "tensor"),
            P("pool", None, "tensor"),
        ),
        check_vma=False,
    )
```

time: 566 us -> 295 us (0.52)
  waiting for transfers between devices: 407 us -> 174 us
  blocking collectives: 29.1 us -> 0 us
  matrix products: 36.7 us -> 16.7 us
  starting transfers between devices: 25.5 us -> 43.7 us
  Pallas kernels: 0 us -> 17.6 us
  other arithmetic: 23.4 us -> 5.97 us
    all_gather x3 -> x1, waiting for transfers between devices: 287 us -> 0.02 us  [shards(): lax.all_gather(paired, 'pool', axis=0, tiled=True)]
    ppermute x0 -> x11, waiting for transfers between devices: none -> 66.2 us  [the longest x8 41.4 us: along_x(): return lax.ppermute(values, 'tensor', pairs)]
    all_to_all x1, waiting for transfers between devices: 114 us -> 51.1 us  [shards(): lax.all_to_all(outgoing, 'pool', split_axis=0, concat_axis=0, tiled=True)]
    all_to_all x1, waiting for transfers between devices: 0.01 us -> 56.5 us  [shards(): lax.all_to_all(spread, 'pool', split_axis=0, concat_axis=0, tiled=True)]
    all_gather x1 -> x0, blocking collectives: 29.1 us -> none  [shards(): lax.all_gather(new_hidden, 'tensor', axis=2, tiled=True)]
    ppermute x0 -> x11, starting transfers between devices: none -> 20.4 us  [the longest x3 10.3 us: across_y(): return lax.ppermute(values, 'tensor', [(s, s ^ 1) for s in range(N_TENSOR)])]
    pallas_call x0 -> x2, Pallas kernels: none -> 17.6 us  [the longest x1 10.6 us: project(): pl.pallas_call(near_kernel, out_shape=(jax.ShapeDtypeStruct((rows, column...]
    dot_general x3 -> x4, matrix products: 29.9 us -> 12.3 us  [the longest x1 4.8 us: pick_rows(): jnp.dot(chosen, table, preferred_element_type=jnp.float32)]
  transfers between devices with their start and end apart: 6 -> 14, of which waited for: 5 -> 8; matrix products, arithmetic and copies ran while one was open for 12% -> 9% of each run, Pallas kernels for 0% -> 4%
where the time goes in v1:
time: 295 us; the launch traced here: 294 us
  waiting for transfers between devices  174 us (59%)
  starting transfers between devices  43.7 us (15%)
  local copies, waits for them, and re-layouts  22 us (7%)
  Pallas kernels  17.6 us (6%)
  matrix products  16.7 us (6%)
  between operations  14.6 us (5%)
  other arithmetic  5.97 us (2%)
    all_to_all x1, waiting for transfers between devices, shards(): lax.all_to_all(spread, 'pool', split_axis=0, concat_axis=0, tiled=True)  56.5 us
    all_to_all x1, waiting for transfers between devices, shards(): lax.all_to_all(outgoing, 'pool', split_axis=0, concat_axis=0, tiled=True)  51.1 us
    ppermute x8, waiting for transfers between devices, along_x(): return lax.ppermute(values, 'tensor', pairs)  41.4 us
    ppermute x3, waiting for transfers between devices, across_y(): return lax.ppermute(values, 'tensor', [(s, s ^ 1) for s in range(N_TENSOR)])  24.8 us
    unnamed x50, local copies, waits for them, and re-layouts  17.8 us
    all_to_all x1, starting transfers between devices, shards(): lax.all_to_all(outgoing, 'pool', split_axis=0, concat_axis=0, tiled=True)  11.9 us
    all_to_all x1, starting transfers between devices, shards(): lax.all_to_all(spread, 'pool', split_axis=0, concat_axis=0, tiled=True)  11.3 us
    pallas_call x1, Pallas kernels, project(): pl.pallas_call(near_kernel, out_shape=(jax.ShapeDtypeStruct((rows, column...  10.6 us
  transfers between devices with their start and end apart: 14, of which 8 were waited for; matrix products, arithmetic and copies ran while one was open for 9% of the time, Pallas kernels for 4%

profile of v1, /device:TPU:1, one launch (start us, length us, event | category | flops | bytes accessed | tf_op | source)
XLA Modules:
  0.0 294.4 jit_solution(12982476556678720071)
XLA Ops:
  7.2 4.1 %fusion.5 = bf16[128,16,640]{2,0,1:T(8,128)(2,1)} fusion(bf16[16,16,8,640]{3,2,0,1:T(8,128)(2,1)} %bitcast.86, s32[128]{0:T(128)S(1)} %fusion.44), kind=kOutput, calls=%fused_computation.7 | convolution fusion | flops 336871424 | bytes 5243392 | tf_op jit(solution)/shard_map/ab,qbc->qac/dot_general | solution.py:242
  11.4 11.3 %all-to-all-start = ((bf16[32,64,640]{2,1,0:T(8,128)(2,1)}), bf16[32,64,640]{2,1,0:T(8,128)(2,1)}, u32[]{:S(2)}, u32[]{:S(2)}) async-start(bf16[32,64,640]{2,1,0:T(8,128)(2,1)} %bitcast.9), calls=%async_computation | async-start | bytes 5242880 | tf_op jit(solution)/shard_map/all_to_all | solution.py:244
  22.8 0.1 copy.51
  22.9 0.1 reduce
  23.0 0.1 select_reduce_fusion.1
  23.2 0.1 iota_add_fusion
  23.3 0.1 add.257
  23.4 0.1 add.262
  23.6 0.1 reshape.410
  23.8 0.1 broadcast_in_dim.110
  23.9 0.2 select_reduce_fusion
  24.1 0.1 iota_add_fusion.1
  24.2 0.1 add.251
  24.4 0.1 select_reduce_fusion.4
  24.5 0.7 pad_maximum_fusion.7
  25.2 1.6 fusion.22
  26.8 0.3 pad_maximum_fusion.4
  27.1 56.5 %all-to-all-done = bf16[32,64,640]{2,1,0:T(8,128)(2,1)} async-done(((bf16[32,64,640]{2,1,0:T(8,128)(2,1)}), bf16[32,64,640]{2,1,0:T(8,128)(2,1)}, u32[]{:S(2)}, u32[]{:S(2)}) %all-to-all-start) | async-done | bytes 2621472 | tf_op jit(solution)/shard_map/all_to_all | solution.py:244
  83.7 4.8 %fusion.8 = bf16[832,640]{1,0:T(8,128)(2,1)S(1)} fusion(bf16[2048,640]{1,0:T(8,128)(2,1)} %bitcast.11, s32[832]{0:T(1024)S(1)} %add.251), kind=kOutput, calls=%fused_computation.12 | convolution fusion | flops 2183274496 | bytes 3689728 | tf_op jit(solution)/shard_map/dot_general | solution.py:178
  88.5 0.2 fusion.18
  88.7 2.7 collective-permute-start
  91.5 1.3 collective-permute-start.1
  92.8 1.5 collective-permute-start.2
  94.2 5.1 %collective-permute-done.1 = bf16[208,640]{1,0:T(8,128)(2,1)S(1)} collective-permute-done((bf16[208,640]{1,0:T(8,128)(2,1)S(1)}, bf16[208,640]{1,0:T(8,128)(2,1)S(1)}, u32[]{:S(2)}, u32[]{:S(2)}) %collective-permute-start.1) | collective-permute-done | bytes 266272 | tf_op jit(solution)/shard_map/ppermute | solution.py:183
  99.3 21.8 %collective-permute-done = bf16[640,640]{1,0:T(8,128)(2,1)S(1)} collective-permute-done((bf16[640,640]{1,0:T(8,128)(2,1)S(1)}, bf16[640,640]{1,0:T(8,128)(2,1)S(1)}, u32[]{:S(2)}, u32[]{:S(2)}) %collective-permute-start) | collective-permute-done | bytes 819232 | tf_op jit(solution)/shard_map/ppermute | solution.py:187
  121.2 0.1 pad_maximum_fusion.two_ref
  121.3 1.2 collective-permute-start.5
  122.5 1.6 collective-permute-start.6
  124.2 4.0 %collective-permute-start.7 = (bf16[624,640]{1,0:T(8,128)(2,1)S(1)}, bf16[624,640]{1,0:T(8,128)(2,1)S(1)}, u32[]{:S(2)}, u32[]{:S(2)}) collective-permute-start(bf16[624,640]{1,0:T(8,128)(2,1)S(1)} %pad_maximum_fusion.3.near_ref), channel_id=1, source_target_pairs={{0,1},{1,0},{2,3},{3,2},{4,5},{5,4},{6,7},{7,6},{8,9},{9,8},{10,11... | collective-permute-start | bytes 2396168 | tf_op jit(solution)/shard_map/ppermute | solution.py:187
  128.2 0.1 collective-permute-start.3
  128.3 2.7 collective-permute-start.4
  130.9 26.7 %collective-permute-done.3 = bf16[104,640]{1,0:T(8,128)(2,1)S(1)} collective-permute-done((bf16[104,640]{1,0:T(8,128)(2,1)S(1)}, bf16[104,640]{1,0:T(8,128)(2,1)S(1)}, u32[]{:S(2)}, u32[]{:S(2)}) %collective-permute-start.3) | collective-permute-done | bytes 133152 | tf_op jit(solution)/shard_map/ppermute | solution.py:183
  157.6 3.0 %collective-permute-done.7.near_across_ref = bf16[624,640]{1,0:T(8,128)(2,1)S(1)} collective-permute-done((bf16[624,640]{1,0:T(8,128)(2,1)S(1)}, bf16[624,640]{1,0:T(8,128)(2,1)S(1)}, u32[]{:S(2)}, u32[]{:S(2)}) %collective-permute-start.7) | collective-permute-done | bytes 798752 | tf_op jit(solution)/shard_map/ppermute | solution.py:187
  160.6 0.9 copy-done.10
  161.6 1.9 collective-permute-start.10
  163.5 1.0 slice.37
  164.7 0.1 copy.49
  164.7 0.1 reshape.404.source_ref
  164.8 0.2 copy.52.live_ref
  165.0 3.6 %collective-permute-start.8 = (bf16[208,640]{1,0:T(8,128)(2,1)S(1)}, bf16[208,640]{1,0:T(8,128)(2,1)S(1)}, u32[]{:S(2)}, u32[]{:S(2)}) collective-permute-start(bf16[208,640]{1,0:T(8,128)(2,1)S(1)} %pad_maximum_fusion.6.far_ref), channel_id=1, source_target_pairs={{0,1},{1,0},{2,3},{3,2},{4,5},{5,4},{6,7},{7,6},{8,9},{9,8},{10,11... | collective-permute-start | bytes 798728 | tf_op jit(solution)/shard_map/ppermute | solution.py:187
  168.7 6.1 %collective-permute-done.10 = bf16[640,640]{1,0:T(8,128)(2,1)S(1)} collective-permute-done((bf16[640,640]{1,0:T(8,128)(2,1)S(1)}, bf16[640,640]{1,0:T(8,128)(2,1)S(1)}, u32[]{:S(2)}, u32[]{:S(2)}) %collective-permute-start.10) | collective-permute-done | bytes 819232 | tf_op jit(solution)/shard_map/ppermute | solution.py:183
  174.7 0.9 copy-done.12
  175.6 3.5 %collective-permute-done.9 = bf16[640,640]{1,0:T(8,128)(2,1)} collective-permute-done((bf16[640,640]{1,0:T(8,128)(2,1)}, bf16[640,640]{1,0:T(8,128)(2,1)}, u32[]{:S(2)}, u32[]{:S(2)}) %collective-permute-start.9) | collective-permute-done | bytes 819232 | tf_op jit(solution)/shard_map/ppermute | solution.py:183
  179.2 1.5 pad_maximum_fusion.1.two_far_ref
  180.7 1.4 copy-done.3
  182.2 1.1 copy-done.5
  183.3 1.4 copy-done.7
  184.7 1.4 copy-done.9
  186.2 1.1 copy-done.11
  187.3 10.6 %shard_map.164 = (f32[848,768]{1,0:T(8,128)S(1)}, f32[848,128]{1,0:T(8,128)S(1)}) custom-call(s32[8]{0:T(128)S(1)} %reshape.404.source_ref, bf16[624,640]{1,0:T(8,128)(2,1)S(1)} %copy-done.5, bf16[624,640]{1,0:T(8,128)(2,1)S(1)} %copy-done.11, bf16[1280,640]{1,0:T(8,128)(2,1)S(1)} %copy-done.3, bf16[1280,640]{1,0:T(8,128)(2,1)S(1)} %copy-done.7, ...), custom_call_target="tpu_custom_call" | custom-call | flops 5001707520 | bytes 16547840 | tf_op jit(solution)/shard_map/pallas_call | solution.py:140
  197.9 7.1 %shard_map.165 = (bf16[32,56,768]{2,1,0:T(8,128)(2,1)S(1)}, bf16[16,768]{1,0:T(8,128)(2,1)S(1)}) custom-call(s32[8]{0:T(128)S(1)} %reshape.404.source_ref, s32[32]{0:T(128)S(1)} %get-tuple-element.25.start_ref, s32[32]{0:T(128)S(1)} %get-tuple-element.26.count_ref, bf16[208,640]{1,0:T(8,128)(2,1)S(1)} %pad_maximum_fusion.6.far_ref, ...), custom_call_target="tpu_custom_call" | custom-call | flops 1667235840 | bytes 8273920 | tf_op jit(solution)/shard_map/pallas_call | solution.py:154
  205.0 1.6 copy-done.1
  206.5 11.9 %all-to-all-start.1 = ((bf16[32,56,768]{2,1,0:T(8,128)(2,1)}), bf16[32,56,768]{2,1,0:T(8,128)(2,1)}, u32[]{:S(2)}, u32[]{:S(2)}) async-start(bf16[32,56,768]{2,1,0:T(8,128)(2,1)} %copy-done.1), calls=%async_computation.1 | async-start | bytes 5505024 | tf_op jit(solution)/shard_map/all_to_all | solution.py:283
  218.5 3.2 %copy.54 = bf16[4,1024,384]{1,2,0:T(8,128)(2,1)S(1)} copy(bf16[4,1024,384]{2,1,0:T(8,128)(2,1)} %param.23) | data formatting | bytes 6291456 | tf_op args[10]
  221.7 4.6 %copy.58 = bf16[4,1024,384]{1,2,0:T(8,128)(2,1)} copy(bf16[4,1024,384]{2,1,0:T(8,128)(2,1)} %param.24) | data formatting | bytes 6291456 | tf_op args[11]
  226.4 0.6 fusion.49
  227.1 0.2 fusion.50
  227.3 0.2 fusion.27
  227.5 2.8 convolution_bitcast_fusion.1
  230.4 0.8 fusion.17
  231.2 51.1 %all-to-all-done.1 = bf16[32,56,768]{2,1,0:T(8,128)(2,1)} async-done(((bf16[32,56,768]{2,1,0:T(8,128)(2,1)}), bf16[32,56,768]{2,1,0:T(8,128)(2,1)}, u32[]{:S(2)}, u32[]{:S(2)}) %all-to-all-start.1) | async-done | bytes 2752544 | tf_op jit(solution)/shard_map/all_to_all | solution.py:283
  282.3 2.0 copy_bitcast_fusion
  284.2 1.7 convolution_convert_fusion.1
  285.9 1.7 convolution_convert_fusion
  (84 shorter events, 1.1 us)
Async XLA Ops:
  7.2 219.2 %copy-start = (bf16[4,2,384]{2,1,0:T(2,128)(2,1)S(1)}, bf16[4,2,384]{2,1,0:T(2,128)(2,1)}, u32[]{:S(2)}) copy-start(bf16[4,2,384]{2,1,0:T(2,128)(2,1)} %param.22) | copy-start | bytes 18436
  11.3 11.5 %copy-start.20 = (s32[16]{0:T(128)S(1)}, s32[16]{0:T(128)}, u32[]{:S(2)}) copy-start(s32[16]{0:T(128)} %param.17) | copy-start | bytes 196
  11.3 11.7 %copy-start.22 = (s32[16]{0:T(128)S(1)}, s32[16]{0:T(128)}, u32[]{:S(2)}) copy-start(s32[16]{0:T(128)} %param.18) | copy-start | bytes 196
  11.3 12.0 %copy-start.21 = (s32[4]{0:T(128)S(1)}, s32[4]{0:T(128)}, u32[]{:S(2)}) copy-start(s32[4]{0:T(128)} %param.25) | copy-start | bytes 52
  11.3 12.4 %copy-start.17 = (s32[16,14]{1,0:T(8,128)S(1)}, s32[16,14]{1,0:T(8,128)}, u32[]{:S(2)}) copy-start(s32[16,14]{1,0:T(8,128)} %param.20) | copy-start | bytes 2692
  11.3 13.0 %copy-start.23 = (s32[32]{0:T(128)S(1)}, s32[32]{0:T(128)}, u32[]{:S(2)}) copy-start(s32[32]{0:T(128)} %param.19) | copy-start | bytes 388
  11.3 13.1 %copy-start.13 = (bf16[160,384]{1,0:T(8,128)(2,1)S(1)}, bf16[160,384]{1,0:T(8,128)(2,1)}, u32[]{:S(2)}) copy-start(bf16[160,384]{1,0:T(8,128)(2,1)} %param.16) | copy-start | bytes 368644
  11.4 13.1 %copy-start.14 = (bf16[160,384]{1,0:T(8,128)(2,1)S(1)}, bf16[160,384]{1,0:T(8,128)(2,1)}, u32[]{:S(2)}) copy-start(bf16[160,384]{1,0:T(8,128)(2,1)} %param.15) | copy-start | bytes 368644
  11.4 72.2 %all-to-all-start = ((bf16[32,64,640]{2,1,0:T(8,128)(2,1)}), bf16[32,64,640]{2,1,0:T(8,128)(2,1)}, u32[]{:S(2)}, u32[]{:S(2)}) async-start(bf16[32,64,640]{2,1,0:T(8,128)(2,1)} %bitcast.9), calls=%async_computation | async-start | bytes 5242880 | tf_op jit(solution)/shard_map/all_to_all | solution.py:244
  22.7 60.9 %copy-start.15 = (bf16[4,2,640]{2,1,0:T(2,128)(2,1)S(1)}, bf16[4,2,640]{2,1,0:T(2,128)(2,1)}, u32[]{:S(2)}) copy-start(bf16[4,2,640]{2,1,0:T(2,128)(2,1)} %param.21) | copy-start | bytes 30724
  22.7 158.0 %all-gather.2.cloned.1.call-start = ((), (), s32[]{:S(2)}) async-start(), calls=%async_computation.2 | async-start | bytes 8110080 | tf_op jit(solution)/shard_map/all_gather | solution.py:274
  88.7 32.4 %collective-permute-start = (bf16[640,640]{1,0:T(8,128)(2,1)S(1)}, bf16[640,640]{1,0:T(8,128)(2,1)S(1)}, u32[]{:S(2)}, u32[]{:S(2)}) collective-permute-start(bf16[640,640]{1,0:T(8,128)(2,1)S(1)} %fusion.18), channel_id=1, source_target_pairs={{0,1},{1,0},{2,3},{3,2},{4,5},{5,4},{6,7},{7,6},{8,9},{9,8},{10,11... | collective-permute-start | bytes 2457608 | tf_op jit(solution)/shard_map/ppermute | solution.py:187
  91.5 7.8 %collective-permute-start.1 = (bf16[208,640]{1,0:T(8,128)(2,1)S(1)}, bf16[208,640]{1,0:T(8,128)(2,1)S(1)}, u32[]{:S(2)}, u32[]{:S(2)}) collective-permute-start(bf16[208,640]{1,0:T(8,128)(2,1)S(1)} %slice.45), channel_id=1, source_target_pairs={{0,2},{1,3},{2,4},{3,5},{4,6},{5,7},{6,0},{7,1},{8,10},{9,11},{10,... | collective-permute-start | bytes 798728 | tf_op jit(solution)/shard_map/ppermute | solution.py:183
  92.8 6.6 %collective-permute-start.2 = (bf16[208,640]{1,0:T(8,128)(2,1)S(1)}, bf16[208,640]{1,0:T(8,128)(2,1)S(1)}, u32[]{:S(2)}, u32[]{:S(2)}) collective-permute-start(bf16[208,640]{1,0:T(8,128)(2,1)S(1)} %slice.45), channel_id=1, source_target_pairs={{0,6},{1,7},{2,0},{3,1},{4,2},{5,3},{6,4},{7,5},{8,14},{9,15},{10,... | collective-permute-start | bytes 798728 | tf_op jit(solution)/shard_map/ppermute | solution.py:183
  121.3 43.2 %copy-start.2 = (bf16[1280,640]{1,0:T(8,128)(2,1)}, bf16[1280,640]{1,0:T(8,128)(2,1)S(1)}, u32[]{:S(2)}) copy-start(bf16[1280,640]{1,0:T(8,128)(2,1)S(1)} %pad_maximum_fusion.two_ref) | copy-start | bytes 4915204
  121.3 40.2 %collective-permute-start.5 = (bf16[1280,640]{1,0:T(8,128)(2,1)S(1)}, bf16[1280,640]{1,0:T(8,128)(2,1)S(1)}, u32[]{:S(2)}, u32[]{:S(2)}) collective-permute-start(bf16[1280,640]{1,0:T(8,128)(2,1)S(1)} %pad_maximum_fusion.two_ref), channel_id=1, source_target_pairs={{0,2},{1,3},{2,4},{3,5},{4,6},{5,7},{6,0},{7,1},{8,10},{9,11},{10,... | collective-permute-start | bytes 4915208 | tf_op jit(solution)/shard_map/ppermute | solution.py:183
  122.5 39.0 %collective-permute-start.6 = (bf16[1280,640]{1,0:T(8,128)(2,1)S(1)}, bf16[1280,640]{1,0:T(8,128)(2,1)S(1)}, u32[]{:S(2)}, u32[]{:S(2)}) collective-permute-start(bf16[1280,640]{1,0:T(8,128)(2,1)S(1)} %pad_maximum_fusion.two_ref), channel_id=1, source_target_pairs={{0,6},{1,7},{2,0},{3,1},{4,2},{5,3},{6,4},{7,5},{8,14},{9,15},{10,... | collective-permute-start | bytes 4915208 | tf_op jit(solution)/shard_map/ppermute | solution.py:183
  124.1 37.4 %copy-start.4 = (bf16[624,640]{1,0:T(8,128)(2,1)}, bf16[624,640]{1,0:T(8,128)(2,1)S(1)}, u32[]{:S(2)}) copy-start(bf16[624,640]{1,0:T(8,128)(2,1)S(1)} %pad_maximum_fusion.3.near_ref) | copy-start | bytes 2396164
  124.1 40.7 %copy-start.16 = (bf16[5120]{0:T(1024)(128)(2,1)S(1)}, bf16[5120]{0:T(1024)(128)(2,1)}, u32[]{:S(2)}) copy-start(bf16[5120]{0:T(1024)(128)(2,1)} %param.14) | copy-start | bytes 30724
  124.2 36.5 %collective-permute-start.7 = (bf16[624,640]{1,0:T(8,128)(2,1)S(1)}, bf16[624,640]{1,0:T(8,128)(2,1)S(1)}, u32[]{:S(2)}, u32[]{:S(2)}) collective-permute-start(bf16[624,640]{1,0:T(8,128)(2,1)S(1)} %pad_maximum_fusion.3.near_ref), channel_id=1, source_target_pairs={{0,1},{1,0},{2,3},{3,2},{4,5},{5,4},{6,7},{7,6},{8,9},{9,8},{10,11... | collective-permute-start | bytes 2396168 | tf_op jit(solution)/shard_map/ppermute | solution.py:187
  128.2 29.4 %collective-permute-start.3 = (bf16[104,640]{1,0:T(8,128)(2,1)S(1)}, bf16[104,640]{1,0:T(8,128)(2,1)S(1)}, u32[]{:S(2)}, u32[]{:S(2)}) collective-permute-start(bf16[104,640]{1,0:T(8,128)(2,1)S(1)} %slice.35), channel_id=1, source_target_pairs={{0,2},{1,3},{2,4},{3,5},{4,6},{5,7},{6,0},{7,1},{8,10},{9,11},{10,... | collective-permute-start | bytes 399368 | tf_op jit(solution)/shard_map/ppermute | solution.py:183
  128.3 29.4 %collective-permute-start.4 = (bf16[104,640]{1,0:T(8,128)(2,1)S(1)}, bf16[104,640]{1,0:T(8,128)(2,1)S(1)}, u32[]{:S(2)}, u32[]{:S(2)}) collective-permute-start(bf16[104,640]{1,0:T(8,128)(2,1)S(1)} %slice.36), channel_id=1, source_target_pairs={{0,6},{1,7},{2,0},{3,1},{4,2},{5,3},{6,4},{7,5},{8,14},{9,15},{10,... | collective-permute-start | bytes 399368 | tf_op jit(solution)/shard_map/ppermute | solution.py:183
  160.6 0.9 copy-start.10
  161.5 2.0 copy-start.6
  161.5 3.0 %copy-start.8 = (bf16[1280,640]{1,0:T(8,128)(2,1)}, bf16[1280,640]{1,0:T(8,128)(2,1)S(1)}, u32[]{:S(2)}) copy-start(bf16[1280,640]{1,0:T(8,128)(2,1)S(1)} %collective-permute-done.6.after_ref) | copy-start | bytes 4915204
  161.6 13.1 %collective-permute-start.10 = (bf16[640,640]{1,0:T(8,128)(2,1)S(1)}, bf16[640,640]{1,0:T(8,128)(2,1)S(1)}, u32[]{:S(2)}, u32[]{:S(2)}) collective-permute-start(bf16[640,640]{1,0:T(8,128)(2,1)S(1)} %slice.38), channel_id=1, source_target_pairs={{0,6},{1,7},{2,0},{3,1},{4,2},{5,3},{6,4},{7,5},{8,14},{9,15},{10,... | collective-permute-start | bytes 2457608 | tf_op jit(solution)/shard_map/ppermute | solution.py:183
  164.5 14.7 %collective-permute-start.9 = (bf16[640,640]{1,0:T(8,128)(2,1)}, bf16[640,640]{1,0:T(8,128)(2,1)}, u32[]{:S(2)}, u32[]{:S(2)}) collective-permute-start(bf16[640,640]{1,0:T(8,128)(2,1)} %slice.37), channel_id=1, source_target_pairs={{0,2},{1,3},{2,4},{3,5},{4,6},{5,7},{6,0},{7,1},{8,10},{9,11},{10,... | collective-permute-start | bytes 2457608 | tf_op jit(solution)/shard_map/ppermute | solution.py:183
  165.0 32.8 %collective-permute-start.8 = (bf16[208,640]{1,0:T(8,128)(2,1)S(1)}, bf16[208,640]{1,0:T(8,128)(2,1)S(1)}, u32[]{:S(2)}, u32[]{:S(2)}) collective-permute-start(bf16[208,640]{1,0:T(8,128)(2,1)S(1)} %pad_maximum_fusion.6.far_ref), channel_id=1, source_target_pairs={{0,1},{1,0},{2,3},{3,2},{4,5},{5,4},{6,7},{7,6},{8,9},{9,8},{10,11... | collective-permute-start | bytes 798728 | tf_op jit(solution)/shard_map/ppermute | solution.py:187
  174.7 0.9 copy-start.12
  180.7 1.4 copy-start.3
  182.2 1.1 copy-start.5
  183.3 1.4 copy-start.7
  184.7 1.4 copy-start.9
  186.2 1.1 copy-start.11
  205.0 1.6 copy-start.1
  206.5 75.7 %all-to-all-start.1 = ((bf16[32,56,768]{2,1,0:T(8,128)(2,1)}), bf16[32,56,768]{2,1,0:T(8,128)(2,1)}, u32[]{:S(2)}, u32[]{:S(2)}) async-start(bf16[32,56,768]{2,1,0:T(8,128)(2,1)} %copy-done.1), calls=%async_computation.1 | async-start | bytes 5505024 | tf_op jit(solution)/shard_map/all_to_all | solution.py:283
  227.1 57.2 %copy-start.18 = (bf16[4,2,384]{2,1,0:T(2,128)(2,1)}, bf16[4,2,384]{2,1,0:T(2,128)(2,1)S(1)}, u32[]{:S(2)}) copy-start(bf16[4,2,384]{2,1,0:T(2,128)(2,1)S(1)} %get-tuple-element.52) | copy-start | bytes 18436
  227.1 57.2 %copy-start.19 = (bf16[4,2,384]{2,1,0:T(2,128)(2,1)}, bf16[4,2,384]{2,1,0:T(2,128)(2,1)S(1)}, u32[]{:S(2)}) copy-start(bf16[4,2,384]{2,1,0:T(2,128)(2,1)S(1)} %get-tuple-element.53) | copy-start | bytes 18436
Sparse Core Ops, SparseCore 0:
  83.7 85.1 all-gather.1

commit v2 on v1

--- a/solution.py
+++ b/solution.py
@@ -57,23 +57,25 @@
     source_ref,
     near_ref,
     near_across_ref,
-    two_ref,
+    lower_ref,
+    lower_across_ref,
     before_ref,
+    before_across_ref,
     after_ref,
+    after_across_ref,
     gain_ref,
     weight_ref,
     total_ref,
     squares_ref,
     scaled_ref,
 ):
-    low_rows = two_ref.shape[0] // 2
-    top = total_ref.shape[0] - low_rows
+    top = near_ref.shape[0] // 3
+    lower = (lower_ref, lower_across_ref, before_ref, before_across_ref, after_ref, after_across_ref)
 
     def pieces_of(step):
         offset, across = step // 2, step % 2
         upper = (near_across_ref if across else near_ref)[offset * top : (offset + 1) * top, :]
-        lower = (two_ref, before_ref, after_ref)[offset][across * low_rows : (across + 1) * low_rows, :]
-        return upper, lower
+        return upper, lower[step][...]
 
     add_slices(range(6), source_ref, gain_ref, weight_ref, pieces_of, scaled_ref, total_ref, squares_ref, False)
 
@@ -84,7 +86,10 @@
     count_ref,
     far_ref,
     far_across_ref,
-    two_far_ref,
+    low_first_ref,
+    low_second_ref,
+    across_first_ref,
+    across_second_ref,
     gain_ref,
     weight_ref,
     begun_ref,
@@ -99,15 +104,14 @@
     squares_ref,
 ):
     rows, columns = begun_ref.shape
-    low_rows = two_far_ref.shape[0] // 2
     total_ref[:rows, :] = begun_ref[...]
     total_ref[rows:, :] = jnp.zeros((KEPT - rows, columns), jnp.float32)
     squares_ref[...] = begun_squares_ref[...]
 
     def pieces_of(step):
-        across = step % 2
-        upper = (far_across_ref if across else far_ref)[...]
-        return upper, two_far_ref[across * low_rows : (across + 1) * low_rows, :]
+        if step % 2:
+            return far_across_ref[...], across_first_ref[...], across_second_ref[...]
+        return far_ref[...], low_first_ref[...], low_second_ref[...]
 
     add_slices(range(6, 8), source_ref, gain_ref, weight_ref, pieces_of, scaled_ref, total_ref, squares_ref, True)
     inverse = lax.rsqrt(jnp.sum(squares_ref[...], axis=1, keepdims=True) / D + epsilon) * live_ref[...]
@@ -132,7 +136,7 @@
 
 
 def project(sources, starts, counts, pieces, weights, gain_wide, live, cosine, sine_part):
-    near, far, near_across, far_across, two, two_before, two_after, two_far = pieces
+    near_pieces, far_pieces = pieces
     rows = live.shape[0]
     columns = weights.shape[2]
     whole = pl.BlockSpec(memory_space=pltpu.VMEM)
@@ -143,21 +147,21 @@
             jax.ShapeDtypeStruct((rows, columns), jnp.float32),
             jax.ShapeDtypeStruct((rows, 128), jnp.float32),
         ),
-        in_specs=[numbers] + [whole] * 7,
+        in_specs=[numbers] + [whole] * 10,
         out_specs=(whole, whole),
         scratch_shapes=[pltpu.VMEM((rows, SLICE), jnp.bfloat16)],
         compiler_params=pltpu.CompilerParams(vmem_limit_bytes=40 * 1024 * 1024),
         cost_estimate=pl.CostEstimate(
             flops=3 * rows * D * columns // 2, bytes_accessed=2 * D * (rows + columns), transcendentals=0
         ),
-    )(sources, near, near_across, two, two_before, two_after, gain_wide, weights)
+    )(sources, *near_pieces, gain_wide, weights)
     return pl.pallas_call(
         far_kernel,
         out_shape=(
             jax.ShapeDtypeStruct((N_POOL, SLOT, columns), jnp.bfloat16),
             jax.ShapeDtypeStruct((TOKENS, columns), jnp.bfloat16),
         ),
-        in_specs=[numbers] * 3 + [whole] * 10,
+        in_specs=[numbers] * 3 + [whole] * 13,
         out_specs=(whole, whole),
         scratch_shapes=[
             pltpu.VMEM((rows, SLICE), jnp.bfloat16),
@@ -168,9 +172,7 @@
         cost_estimate=pl.CostEstimate(
             flops=rows * D * columns // 2, bytes_accessed=D * (rows + columns), transcendentals=0
         ),
-    )(
-        sources, starts, counts, far, far_across, two_far, gain_wide, weights, total, squares, live, cosine, sine_part
-    )
+    )(sources, starts, counts, *far_pieces, gain_wide, weights, total, squares, live, cosine, sine_part)
 
 
 def pick_rows(index, table):
@@ -187,24 +189,31 @@
     return lax.ppermute(values, "tensor", [(s, s ^ 1) for s in range(N_TENSOR)])
 
 
-def far_x(before, after, rows):
-    return jnp.concatenate([along_x(before[:rows], 1), along_x(after[rows:], -1)], axis=0)
-
-
-def gather_rows(own):
+def far_x(before, after):
+    half = before.shape[0] // 2
+    return along_x(before[:half], 1), along_x(after[half:], -1)
+
+
+def gather_rows(own, weights):
     upper, lower = own[:X_FIRST], own[X_FIRST:]
-    other = across_y(lower)
-    before, after = along_x(upper, 1), along_x(upper, -1)
-    other, before, after = lax.optimization_barrier((other, before, after))
-    near = jnp.concatenate([upper, before, after], axis=0)
-    two = jnp.concatenate([lower, other], axis=0)
-    far = far_x(before, after, X_FIRST // 2)
-    two_before, two_after = along_x(two, 1), along_x(two, -1)
+    lower_across = across_y(lower)
+    upper_before, upper_after = along_x(upper, 1), along_x(upper, -1)
+    before, after = along_x(lower, 1), along_x(lower, -1)
+    lower_across, upper_before, upper_after, before, after = lax.optimization_barrier(
+        (lower_across, upper_before, upper_after, before, after)
+    )
+    before_across, after_across = along_x(lower_across, 1), along_x(lower_across, -1)
+    near = jnp.concatenate([upper, upper_before, upper_after], axis=0)
     near_across = across_y(near)
-    far, two_before, two_after, near_across = lax.optimization_barrier((far, two_before, two_after, near_across))
+    far = jnp.concatenate(far_x(upper_before, upper_after), axis=0)
+    lower_far = far_x(before, after)
+    far, lower_far, before_across, after_across, near_across, weights = lax.optimization_barrier(
+        (far, lower_far, before_across, after_across, near_across, weights)
+    )
     far_across = across_y(far)
-    two_far = far_x(two_before, two_after, lower.shape[0])
-    return near, far, near_across, far_across, two, two_before, two_after, two_far
+    across_far = far_x(before_across, after_across)
+    near_pieces = (near, near_across, lower, lower_across, before, before_across, after, after_across)
+    return (near_pieces, (far, far_across, *lower_far, *across_far)), weights
 
 
 def shards(
@@ -277,8 +286,9 @@
     )
     own = pick_rows(my_rows, incoming.reshape(N_POOL * REQS * SHARE, slice_width))
     own = jnp.concatenate([own, token_rows], axis=0)
+    pieces, weights = gather_rows(own, weights)
     outgoing, fresh = project(
-        sources, group_start, group_rows, gather_rows(own), weights, gain_wide, live, cosine, sine_part
+        sources, group_start, group_rows, pieces, weights, gain_wide, live, cosine, sine_part
     )
     arrived = lax.all_to_all(outgoing, "pool", split_axis=0, concat_axis=0, tiled=True)
     pairs = arrived.reshape(N_POOL, GBLK // 2, 2 * SHARE, 2 * head_width).transpose(1, 0, 2, 3)

time: 295 us -> 280 us (0.949)
  waiting for transfers between devices: 174 us -> 160 us
  Pallas kernels: 17.6 us -> 20.6 us
    ppermute x3, waiting for transfers between devices: 24.8 us -> 10.1 us  [across_y(): return lax.ppermute(values, 'tensor', [(s, s ^ 1) for s in range(N_TENSOR)])]
    all_gather x1, waiting for transfers between devices: 0.02 us -> 11.3 us  [shards(): lax.all_gather(paired, 'pool', axis=0, tiled=True)]
    ppermute x8 -> x12, waiting for transfers between devices: 41.4 us -> 34.8 us  [along_x(): return lax.ppermute(values, 'tensor', pairs)]
    unnamed x50 -> x34, local copies, waits for them, and re-layouts: 17.8 us -> 11.7 us
    ppermute x8 -> x12, starting transfers between devices: 10.2 us -> 16.2 us  [along_x(): return lax.ppermute(values, 'tensor', pairs)]
    all_to_all x1, starting transfers between devices: 11.9 us -> 6.86 us  [shards(): lax.all_to_all(outgoing, 'pool', split_axis=0, concat_axis=0, tiled=True)]
    slice x4 -> x6, local copies, waits for them, and re-layouts: 1.06 us -> 5.35 us  [far_x(): return (along_x(before[:half], 1), along_x(after[half:], -1))]
    all_to_all x1, waiting for transfers between devices: 51.1 us -> 47.6 us  [shards(): lax.all_to_all(outgoing, 'pool', split_axis=0, concat_axis=0, tiled=True)]
  transfers between devices with their start and end apart: 14 -> 18, of which waited for: 8 -> 8; matrix products, arithmetic and copies ran while one was open for 9% -> 11% of each run, Pallas kernels for 4% -> 4%
where the time goes in v2:
time: 280 us
  waiting for transfers between devices  160 us (57%)
  starting transfers between devices  41.9 us (15%)
  Pallas kernels  20.6 us (7%)
  local copies, waits for them, and re-layouts  20.2 us (7%)
  matrix products  16.8 us (6%)
  between operations  14.4 us (5%)
  other arithmetic  5.26 us (2%)
    all_to_all x1, waiting for transfers between devices, shards(): lax.all_to_all(spread, 'pool', split_axis=0, concat_axis=0, tiled=True)  56.4 us
    all_to_all x1, waiting for transfers between devices, shards(): lax.all_to_all(outgoing, 'pool', split_axis=0, concat_axis=0, tiled=True)  47.6 us
    ppermute x12, waiting for transfers between devices, along_x(): return lax.ppermute(values, 'tensor', pairs)  34.8 us
    ppermute x12, starting transfers between devices, along_x(): return lax.ppermute(values, 'tensor', pairs)  16.2 us
    unnamed x34, local copies, waits for them, and re-layouts  11.7 us
    pallas_call x1, Pallas kernels, project(): pl.pallas_call(near_kernel, out_shape=(jax.ShapeDtypeStruct((rows, column...  11.5 us
    all_gather x1, waiting for transfers between devices, shards(): lax.all_gather(paired, 'pool', axis=0, tiled=True)  11.3 us
    all_to_all x1, starting transfers between devices, shards(): lax.all_to_all(spread, 'pool', split_axis=0, concat_axis=0, tiled=True)  11.3 us
  transfers between devices with their start and end apart: 18, of which 8 were waited for; matrix products, arithmetic and copies ran while one was open for 11% of the time, Pallas kernels for 4%

profile of v2, /device:TPU:1, one launch (start us, length us, event | category | flops | bytes accessed | tf_op | source)
XLA Modules:
  0.0 279.6 jit_solution(8601250852083457303)
XLA Ops:
  7.2 4.1 %fusion.5 = bf16[128,16,640]{2,0,1:T(8,128)(2,1)} fusion(bf16[16,16,8,640]{3,2,0,1:T(8,128)(2,1)} %bitcast.87, s32[128]{0:T(128)S(1)} %fusion.44), kind=kOutput, calls=%fused_computation.7 | convolution fusion | flops 336871424 | bytes 5243392 | tf_op jit(solution)/shard_map/ab,qbc->qac/dot_general | solution.py:251
  11.4 11.3 %all-to-all-start = ((bf16[32,64,640]{2,1,0:T(8,128)(2,1)}), bf16[32,64,640]{2,1,0:T(8,128)(2,1)S(1)}, u32[]{:S(2)}, u32[]{:S(2)}) async-start(bf16[32,64,640]{2,1,0:T(8,128)(2,1)} %bitcast.9), calls=%async_computation | async-start | bytes 5242880 | tf_op jit(solution)/shard_map/all_to_all | solution.py:253
  22.7 0.1 copy.51
  22.9 0.1 reduce
  23.0 0.1 select_reduce_fusion.1
  23.1 0.1 iota_add_fusion
  23.2 0.1 add.257
  23.4 0.1 add.262
  23.6 0.1 reshape.410
  23.7 0.1 broadcast_in_dim.110
  23.8 0.2 select_reduce_fusion
  24.0 0.1 iota_add_fusion.1
  24.1 0.1 add.251
  24.3 0.1 select_reduce_fusion.4
  24.4 0.7 pad_maximum_fusion.5
  25.2 1.6 fusion.22
  26.8 0.3 pad_maximum_fusion.2
  27.1 56.4 %all-to-all-done = bf16[32,64,640]{2,1,0:T(8,128)(2,1)S(1)} async-done(((bf16[32,64,640]{2,1,0:T(8,128)(2,1)}), bf16[32,64,640]{2,1,0:T(8,128)(2,1)S(1)}, u32[]{:S(2)}, u32[]{:S(2)}) %all-to-all-start) | async-done | bytes 2621472 | tf_op jit(solution)/shard_map/all_to_all | solution.py:253
  83.6 3.1 %fusion.8 = bf16[832,640]{1,0:T(8,128)(2,1)S(1)} fusion(bf16[2048,640]{1,0:T(8,128)(2,1)S(1)} %bitcast.86, s32[832]{0:T(1024)S(1)} %add.251), kind=kOutput, calls=%fused_computation.10 | convolution fusion | flops 2183274496 | bytes 3689728 | tf_op jit(solution)/shard_map/dot_general | solution.py:180
  86.7 0.2 fusion.18.lower_ref
  86.9 2.7 collective-permute-start
  89.6 1.2 collective-permute-start.3
  90.8 1.5 collective-permute-start.4
  92.3 0.1 collective-permute-start.1
  92.4 2.7 collective-permute-start.2
  95.1 20.0 %collective-permute-done.1 = bf16[208,640]{1,0:T(8,128)(2,1)S(1)} collective-permute-done((bf16[208,640]{1,0:T(8,128)(2,1)S(1)}, bf16[208,640]{1,0:T(8,128)(2,1)S(1)}, u32[]{:S(2)}, u32[]{:S(2)}) %collective-permute-start.1) | collective-permute-done | bytes 266272 | tf_op jit(solution)/shard_map/ppermute | solution.py:185
  115.0 2.5 collective-permute-done.lower_across_ref
  117.5 2.5 collective-permute-start.10
  120.1 3.9 %collective-permute-start.11 = (bf16[624,640]{1,0:T(8,128)(2,1)S(1)}, bf16[624,640]{1,0:T(8,128)(2,1)}, u32[]{:S(2)}, u32[]{:S(2)}) collective-permute-start(bf16[624,640]{1,0:T(8,128)(2,1)S(1)} %pad_maximum_fusion.1.near_ref), channel_id=1, source_target_pairs={{0,1},{1,0},{2,3},{3,2},{4,5},{5,4},{6,7},{7,6},{8,9},{9,8},{10,11... | collective-permute-start | bytes 2396168 | tf_op jit(solution)/shard_map/ppermute | solution.py:189
  124.0 0.7 slice.41
  124.7 0.7 collective-permute-start.5
  125.5 2.0 collective-permute-start.6
  127.6 0.8 slice.43
  128.4 1.8 slice.44
  130.2 8.6 %collective-permute-done.5 = bf16[104,640]{1,0:T(8,128)(2,1)} collective-permute-done((bf16[104,640]{1,0:T(8,128)(2,1)}, bf16[104,640]{1,0:T(8,128)(2,1)}, u32[]{:S(2)}, u32[]{:S(2)}) %collective-permute-start.5) | collective-permute-done | bytes 133152 | tf_op jit(solution)/shard_map/ppermute | solution.py:185
  138.8 2.7 collective-permute-start.8
  141.5 0.1 copy.49
  141.6 0.1 reshape.404.source_ref
  141.7 0.2 copy.52.live_ref
  141.9 1.0 pad_maximum_fusion.4.far_ref
  142.9 6.2 %collective-permute-done.7.low_first_ref = bf16[320,640]{1,0:T(8,128)(2,1)} collective-permute-done((bf16[320,640]{1,0:T(8,128)(2,1)}, bf16[320,640]{1,0:T(8,128)(2,1)}, u32[]{:S(2)}, u32[]{:S(2)}) %collective-permute-start.7) | collective-permute-done | bytes 409632 | tf_op jit(solution)/shard_map/ppermute | solution.py:185
  149.1 7.6 %collective-permute-done.11.near_across_ref = bf16[624,640]{1,0:T(8,128)(2,1)} collective-permute-done((bf16[624,640]{1,0:T(8,128)(2,1)S(1)}, bf16[624,640]{1,0:T(8,128)(2,1)}, u32[]{:S(2)}, u32[]{:S(2)}) %collective-permute-start.11) | collective-permute-done | bytes 798752 | tf_op jit(solution)/shard_map/ppermute | solution.py:189
  156.7 11.3 %all-gather.2.cloned.1.call-done = bf16[5120,768]{1,0:T(8,128)(2,1)} async-done(((bf16[160,768]{1,0:T(8,128)(2,1)}), bf16[5120,768]{1,0:T(8,128)(2,1)}) %all-gather.2.cloned.1.call-update) | async-done | bytes 7864336 | tf_op jit(solution)/shard_map/all_gather | solution.py:283
  168.1 1.0 slice.45
  169.1 1.1 collective-permute-start.13
  170.3 1.0 slice.46
  171.3 1.7 collective-permute-start.14
  173.0 0.9 collective-permute-start.12
  173.9 1.1 copy-done.2
  175.0 1.1 copy-done.4
  176.2 11.5 %shard_map.164 = (f32[848,768]{1,0:T(8,128)S(1)}, f32[848,128]{1,0:T(8,128)S(1)}) custom-call(s32[8]{0:T(128)S(1)} %reshape.404.source_ref, bf16[624,640]{1,0:T(8,128)(2,1)S(1)} %pad_maximum_fusion.1.near_ref, bf16[624,640]{1,0:T(8,128)(2,1)} %collective-permute-done.11.near_across_ref, bf16[640,640]{1,0:T(8,128)(2,1)S(1)} %fusion.18.lower_ref, ...), custom_call_target="tpu_custom_call" | custom-call | flops 5001707520 | bytes 16547840 | tf_op jit(solution)/shard_map/pallas_call | solution.py:144
  187.7 9.1 %shard_map.165 = (bf16[32,56,768]{2,1,0:T(8,128)(2,1)}, bf16[16,768]{1,0:T(8,128)(2,1)S(1)}) custom-call(s32[8]{0:T(128)S(1)} %reshape.404.source_ref, s32[32]{0:T(128)S(1)} %get-tuple-element.30.start_ref, s32[32]{0:T(128)S(1)} %get-tuple-element.31.count_ref, bf16[208,640]{1,0:T(8,128)(2,1)S(1)} %pad_maximum_fusion.4.far_ref, ...), custom_call_target="tpu_custom_call" | custom-call | flops 1667235840 | bytes 8273920 | tf_op jit(solution)/shard_map/pallas_call | solution.py:158
  196.8 6.9 %all-to-all-start.1 = ((bf16[32,56,768]{2,1,0:T(8,128)(2,1)}), bf16[32,56,768]{2,1,0:T(8,128)(2,1)}, u32[]{:S(2)}, u32[]{:S(2)}) async-start(bf16[32,56,768]{2,1,0:T(8,128)(2,1)} %get-tuple-element.53), calls=%async_computation.1 | async-start | bytes 5505024 | tf_op jit(solution)/shard_map/all_to_all | solution.py:293
  203.7 4.7 %copy.54 = bf16[4,1024,384]{1,2,0:T(8,128)(2,1)} copy(bf16[4,1024,384]{2,1,0:T(8,128)(2,1)} %param.23) | data formatting | bytes 6291456 | tf_op args[10]
  208.4 4.7 %copy.58 = bf16[4,1024,384]{1,2,0:T(8,128)(2,1)} copy(bf16[4,1024,384]{2,1,0:T(8,128)(2,1)} %param.24) | data formatting | bytes 6291456 | tf_op args[11]
  213.2 2.5 fusion.49
  215.7 0.2 fusion.50
  215.9 0.2 fusion.27
  216.1 2.8 %convolution_bitcast_fusion.1 = f32[4,2,3,128]{3,1,2,0:T(2,128)S(1)} fusion(bf16[4,1024,3,128]{1,3,2,0:T(8,128)(2,1)} %bitcast.85, f32[4,2,3,1024]{3,1,2,0:T(2,128)S(1)} %get-tuple-element.72, f32[4,2,3]{1,2,0:T(4,128)S(1)} %add.267, f32[4,2,3]{1,2,0:T(4,128)S(1)} %max.7), kind=kOutput, calls=%fused_computation.18 | convolution fusion | flops 6365184 | bytes 3256512 | tf_op jit(solution)/shard_map/rshc,rchd->rshd/dot_general | solution.py:343
  219.0 0.8 fusion.17
  219.8 47.6 %all-to-all-done.1 = bf16[32,56,768]{2,1,0:T(8,128)(2,1)} async-done(((bf16[32,56,768]{2,1,0:T(8,128)(2,1)}), bf16[32,56,768]{2,1,0:T(8,128)(2,1)}, u32[]{:S(2)}, u32[]{:S(2)}) %all-to-all-start.1) | async-done | bytes 2752544 | tf_op jit(solution)/shard_map/all_to_all | solution.py:293
  267.4 2.0 copy_bitcast_fusion
  269.4 1.7 convolution_convert_fusion.1
  271.0 1.7 convolution_convert_fusion
  (76 shorter events, 1.0 us)
Async XLA Ops:
  7.2 206.0 %copy-start = (bf16[4,2,384]{2,1,0:T(2,128)(2,1)S(1)}, bf16[4,2,384]{2,1,0:T(2,128)(2,1)}, u32[]{:S(2)}) copy-start(bf16[4,2,384]{2,1,0:T(2,128)(2,1)} %param.22) | copy-start | bytes 18436
  11.3 11.4 %copy-start.12 = (s32[16]{0:T(128)S(1)}, s32[16]{0:T(128)}, u32[]{:S(2)}) copy-start(s32[16]{0:T(128)} %param.17) | copy-start | bytes 196
  11.3 11.7 %copy-start.14 = (s32[16]{0:T(128)S(1)}, s32[16]{0:T(128)}, u32[]{:S(2)}) copy-start(s32[16]{0:T(128)} %param.18) | copy-start | bytes 196
  11.3 12.0 %copy-start.13 = (s32[4]{0:T(128)S(1)}, s32[4]{0:T(128)}, u32[]{:S(2)}) copy-start(s32[4]{0:T(128)} %param.25) | copy-start | bytes 52
  11.3 12.4 %copy-start.9 = (s32[16,14]{1,0:T(8,128)S(1)}, s32[16,14]{1,0:T(8,128)}, u32[]{:S(2)}) copy-start(s32[16,14]{1,0:T(8,128)} %param.20) | copy-start | bytes 2692
  11.3 13.0 %copy-start.15 = (s32[32]{0:T(128)S(1)}, s32[32]{0:T(128)}, u32[]{:S(2)}) copy-start(s32[32]{0:T(128)} %param.19) | copy-start | bytes 388
  11.3 13.1 %copy-start.5 = (bf16[160,384]{1,0:T(8,128)(2,1)S(1)}, bf16[160,384]{1,0:T(8,128)(2,1)}, u32[]{:S(2)}) copy-start(bf16[160,384]{1,0:T(8,128)(2,1)} %param.16) | copy-start | bytes 368644
  11.4 13.1 %copy-start.6 = (bf16[160,384]{1,0:T(8,128)(2,1)S(1)}, bf16[160,384]{1,0:T(8,128)(2,1)}, u32[]{:S(2)}) copy-start(bf16[160,384]{1,0:T(8,128)(2,1)} %param.15) | copy-start | bytes 368644
  11.4 72.1 %all-to-all-start = ((bf16[32,64,640]{2,1,0:T(8,128)(2,1)}), bf16[32,64,640]{2,1,0:T(8,128)(2,1)S(1)}, u32[]{:S(2)}, u32[]{:S(2)}) async-start(bf16[32,64,640]{2,1,0:T(8,128)(2,1)} %bitcast.9), calls=%async_computation | async-start | bytes 5242880 | tf_op jit(solution)/shard_map/all_to_all | solution.py:253
  22.7 60.8 %copy-start.7 = (bf16[4,2,640]{2,1,0:T(2,128)(2,1)S(1)}, bf16[4,2,640]{2,1,0:T(2,128)(2,1)}, u32[]{:S(2)}) copy-start(bf16[4,2,640]{2,1,0:T(2,128)(2,1)} %param.21) | copy-start | bytes 30724
  22.7 145.4 %all-gather.2.cloned.1.call-start = ((), (), s32[]{:S(2)}) async-start(), calls=%async_computation.2 | async-start | bytes 8110080 | tf_op jit(solution)/shard_map/all_gather | solution.py:283
  86.9 54.8 %copy-start.8 = (bf16[5120]{0:T(1024)(128)(2,1)S(1)}, bf16[5120]{0:T(1024)(128)(2,1)}, u32[]{:S(2)}) copy-start(bf16[5120]{0:T(1024)(128)(2,1)} %param.14) | copy-start | bytes 30724
  86.9 30.6 %collective-permute-start = (bf16[640,640]{1,0:T(8,128)(2,1)S(1)}, bf16[640,640]{1,0:T(8,128)(2,1)}, u32[]{:S(2)}, u32[]{:S(2)}) collective-permute-start(bf16[640,640]{1,0:T(8,128)(2,1)S(1)} %fusion.18.lower_ref), channel_id=1, source_target_pairs={{0,1},{1,0},{2,3},{3,2},{4,5},{5,4},{6,7},{7,6},{8,9},{9,8},{10,11... | collective-permute-start | bytes 2457608 | tf_op jit(solution)/shard_map/ppermute | solution.py:189
  89.6 27.9 %collective-permute-start.3 = (bf16[640,640]{1,0:T(8,128)(2,1)S(1)}, bf16[640,640]{1,0:T(8,128)(2,1)S(1)}, u32[]{:S(2)}, u32[]{:S(2)}) collective-permute-start(bf16[640,640]{1,0:T(8,128)(2,1)S(1)} %fusion.18.lower_ref), channel_id=1, source_target_pairs={{0,2},{1,3},{2,4},{3,5},{4,6},{5,7},{6,0},{7,1},{8,10},{9,11},{10,... | collective-permute-start | bytes 2457608 | tf_op jit(solution)/shard_map/ppermute | solution.py:185
  90.8 26.7 %collective-permute-start.4 = (bf16[640,640]{1,0:T(8,128)(2,1)S(1)}, bf16[640,640]{1,0:T(8,128)(2,1)S(1)}, u32[]{:S(2)}, u32[]{:S(2)}) collective-permute-start(bf16[640,640]{1,0:T(8,128)(2,1)S(1)} %fusion.18.lower_ref), channel_id=1, source_target_pairs={{0,6},{1,7},{2,0},{3,1},{4,2},{5,3},{6,4},{7,5},{8,14},{9,15},{10,... | collective-permute-start | bytes 2457608 | tf_op jit(solution)/shard_map/ppermute | solution.py:185
  92.3 22.7 %collective-permute-start.1 = (bf16[208,640]{1,0:T(8,128)(2,1)S(1)}, bf16[208,640]{1,0:T(8,128)(2,1)S(1)}, u32[]{:S(2)}, u32[]{:S(2)}) collective-permute-start(bf16[208,640]{1,0:T(8,128)(2,1)S(1)} %slice.53), channel_id=1, source_target_pairs={{0,2},{1,3},{2,4},{3,5},{4,6},{5,7},{6,0},{7,1},{8,10},{9,11},{10,... | collective-permute-start | bytes 798728 | tf_op jit(solution)/shard_map/ppermute | solution.py:185
  92.4 22.6 %collective-permute-start.2 = (bf16[208,640]{1,0:T(8,128)(2,1)S(1)}, bf16[208,640]{1,0:T(8,128)(2,1)S(1)}, u32[]{:S(2)}, u32[]{:S(2)}) collective-permute-start(bf16[208,640]{1,0:T(8,128)(2,1)S(1)} %slice.53), channel_id=1, source_target_pairs={{0,6},{1,7},{2,0},{3,1},{4,2},{5,3},{6,4},{7,5},{8,14},{9,15},{10,... | collective-permute-start | bytes 798728 | tf_op jit(solution)/shard_map/ppermute | solution.py:185
  117.5 24.1 %copy-start.1 = (bf16[640,640]{1,0:T(8,128)(2,1)}, bf16[640,640]{1,0:T(8,128)(2,1)S(1)}, u32[]{:S(2)}) copy-start(bf16[640,640]{1,0:T(8,128)(2,1)S(1)} %collective-permute-done.3.before_ref) | copy-start | bytes 2457604
  117.5 2.6 copy-start.3
  117.5 39.2 %collective-permute-start.10 = (bf16[640,640]{1,0:T(8,128)(2,1)}, bf16[640,640]{1,0:T(8,128)(2,1)}, u32[]{:S(2)}, u32[]{:S(2)}) collective-permute-start(bf16[640,640]{1,0:T(8,128)(2,1)} %collective-permute-done.lower_across_ref), channel_id=1, source_target_pairs={{0,6},{1,7},{2,0},{3,1},{4,2},{5,3},{6,4},{7,5},{8,14},{9,15},{10,... | collective-permute-start | bytes 2457608 | tf_op jit(solution)/shard_map/ppermute | solution.py:185
  120.1 36.7 %collective-permute-start.9 = (bf16[640,640]{1,0:T(8,128)(2,1)}, bf16[640,640]{1,0:T(8,128)(2,1)}, u32[]{:S(2)}, u32[]{:S(2)}) collective-permute-start(bf16[640,640]{1,0:T(8,128)(2,1)} %collective-permute-done.lower_across_ref), channel_id=1, source_target_pairs={{0,2},{1,3},{2,4},{3,5},{4,6},{5,7},{6,0},{7,1},{8,10},{9,11},{10,... | collective-permute-start | bytes 2457608 | tf_op jit(solution)/shard_map/ppermute | solution.py:185
  120.1 36.6 %collective-permute-start.11 = (bf16[624,640]{1,0:T(8,128)(2,1)S(1)}, bf16[624,640]{1,0:T(8,128)(2,1)}, u32[]{:S(2)}, u32[]{:S(2)}) collective-permute-start(bf16[624,640]{1,0:T(8,128)(2,1)S(1)} %pad_maximum_fusion.1.near_ref), channel_id=1, source_target_pairs={{0,1},{1,0},{2,3},{3,2},{4,5},{5,4},{6,7},{7,6},{8,9},{9,8},{10,11... | collective-permute-start | bytes 2396168 | tf_op jit(solution)/shard_map/ppermute | solution.py:189
  124.7 14.1 %collective-permute-start.5 = (bf16[104,640]{1,0:T(8,128)(2,1)}, bf16[104,640]{1,0:T(8,128)(2,1)}, u32[]{:S(2)}, u32[]{:S(2)}) collective-permute-start(bf16[104,640]{1,0:T(8,128)(2,1)} %slice.41), channel_id=1, source_target_pairs={{0,2},{1,3},{2,4},{3,5},{4,6},{5,7},{6,0},{7,1},{8,10},{9,11},{10,... | collective-permute-start | bytes 399368 | tf_op jit(solution)/shard_map/ppermute | solution.py:185
  125.5 13.3 %collective-permute-start.6 = (bf16[104,640]{1,0:T(8,128)(2,1)S(1)}, bf16[104,640]{1,0:T(8,128)(2,1)}, u32[]{:S(2)}, u32[]{:S(2)}) collective-permute-start(bf16[104,640]{1,0:T(8,128)(2,1)S(1)} %slice.42), channel_id=1, source_target_pairs={{0,6},{1,7},{2,0},{3,1},{4,2},{5,3},{6,4},{7,5},{8,14},{9,15},{10,... | collective-permute-start | bytes 399368 | tf_op jit(solution)/shard_map/ppermute | solution.py:185
  138.8 10.3 %collective-permute-start.7 = (bf16[320,640]{1,0:T(8,128)(2,1)}, bf16[320,640]{1,0:T(8,128)(2,1)}, u32[]{:S(2)}, u32[]{:S(2)}) collective-permute-start(bf16[320,640]{1,0:T(8,128)(2,1)} %slice.43), channel_id=1, source_target_pairs={{0,2},{1,3},{2,4},{3,5},{4,6},{5,7},{6,0},{7,1},{8,10},{9,11},{10,... | collective-permute-start | bytes 1228808 | tf_op jit(solution)/shard_map/ppermute | solution.py:185
  138.8 10.3 %collective-permute-start.8 = (bf16[320,640]{1,0:T(8,128)(2,1)}, bf16[320,640]{1,0:T(8,128)(2,1)}, u32[]{:S(2)}, u32[]{:S(2)}) collective-permute-start(bf16[320,640]{1,0:T(8,128)(2,1)} %slice.44), channel_id=1, source_target_pairs={{0,6},{1,7},{2,0},{3,1},{4,2},{5,3},{6,4},{7,5},{8,14},{9,15},{10,... | collective-permute-start | bytes 1228808 | tf_op jit(solution)/shard_map/ppermute | solution.py:185
  169.1 18.6 %collective-permute-start.13 = (bf16[320,640]{1,0:T(8,128)(2,1)S(1)}, bf16[320,640]{1,0:T(8,128)(2,1)S(1)}, u32[]{:S(2)}, u32[]{:S(2)}) collective-permute-start(bf16[320,640]{1,0:T(8,128)(2,1)S(1)} %slice.45), channel_id=1, source_target_pairs={{0,2},{1,3},{2,4},{3,5},{4,6},{5,7},{6,0},{7,1},{8,10},{9,11},{10,... | collective-permute-start | bytes 1228808 | tf_op jit(solution)/shard_map/ppermute | solution.py:185
  171.3 16.4 %collective-permute-start.14 = (bf16[320,640]{1,0:T(8,128)(2,1)S(1)}, bf16[320,640]{1,0:T(8,128)(2,1)S(1)}, u32[]{:S(2)}, u32[]{:S(2)}) collective-permute-start(bf16[320,640]{1,0:T(8,128)(2,1)S(1)} %slice.46), channel_id=1, source_target_pairs={{0,6},{1,7},{2,0},{3,1},{4,2},{5,3},{6,4},{7,5},{8,14},{9,15},{10,... | collective-permute-start | bytes 1228808 | tf_op jit(solution)/shard_map/ppermute | solution.py:185
  173.0 14.7 %collective-permute-start.12 = (bf16[208,640]{1,0:T(8,128)(2,1)S(1)}, bf16[208,640]{1,0:T(8,128)(2,1)S(1)}, u32[]{:S(2)}, u32[]{:S(2)}) collective-permute-start(bf16[208,640]{1,0:T(8,128)(2,1)S(1)} %pad_maximum_fusion.4.far_ref), channel_id=1, source_target_pairs={{0,1},{1,0},{2,3},{3,2},{4,5},{5,4},{6,7},{7,6},{8,9},{9,8},{10,11... | collective-permute-start | bytes 798728 | tf_op jit(solution)/shard_map/ppermute | solution.py:189
  173.9 1.1 copy-start.2
  175.0 1.1 copy-start.4
  196.8 70.5 %all-to-all-start.1 = ((bf16[32,56,768]{2,1,0:T(8,128)(2,1)}), bf16[32,56,768]{2,1,0:T(8,128)(2,1)}, u32[]{:S(2)}, u32[]{:S(2)}) async-start(bf16[32,56,768]{2,1,0:T(8,128)(2,1)} %get-tuple-element.53), calls=%async_computation.1 | async-start | bytes 5505024 | tf_op jit(solution)/shard_map/all_to_all | solution.py:293
  215.7 53.7 %copy-start.10 = (bf16[4,2,384]{2,1,0:T(2,128)(2,1)}, bf16[4,2,384]{2,1,0:T(2,128)(2,1)S(1)}, u32[]{:S(2)}) copy-start(bf16[4,2,384]{2,1,0:T(2,128)(2,1)S(1)} %get-tuple-element.62) | copy-start | bytes 18436
  215.7 53.7 %copy-start.11 = (bf16[4,2,384]{2,1,0:T(2,128)(2,1)}, bf16[4,2,384]{2,1,0:T(2,128)(2,1)S(1)}, u32[]{:S(2)}) copy-start(bf16[4,2,384]{2,1,0:T(2,128)(2,1)S(1)} %get-tuple-element.63) | copy-start | bytes 18436
Sparse Core Ops, SparseCore 0:
  83.6 84.4 all-gather.1
